TPU v7x, 32 devices: a whole 2x2x4 slice. The times are simulated.
32 devices in a mesh: section: 2 (over y), row: 4 (over x, core), col: 4 (over z).
Axes of the slice: x: 2, y: 2, z: 4, core: 2. Of those that a mesh axis runs over, the one named last changes fastest.
Arguments:
- x_down: bfloat16 [2, 1024, 8192], P('section', 'row', 'col'), may hold values from -30 to 30
- gain_down: float32 [2, 8192], P('section', 'col'), may hold values from 0.1 to 1.9
- wq_down: bfloat16 [2, 8192, 4096], P('section', 'col', 'row'), may hold values from -2 to 2
- wk_down: bfloat16 [2, 8192, 512], P('section', 'col', 'row'), may hold values from -1 to 1
- wv_down: bfloat16 [2, 8192, 512], P('section', 'col', 'row'), may hold values from -0.0625 to 0.0625
- wo_down: bfloat16 [2, 4096, 8192], P('section', 'row', 'col'), may hold values from -0.09375 to 0.09375
- x_up: bfloat16 [2, 1024, 8192], P('section', 'row', 'col'), may hold values from -30 to 30
- gain_up: float32 [2, 8192], P('section', 'col'), may hold values from 0.1 to 1.9
- wq_up: bfloat16 [2, 8192, 4096], P('section', 'col', 'row'), may hold values from -2 to 2
- wk_up: bfloat16 [2, 8192, 512], P('section', 'col', 'row'), may hold values from -1 to 1
- wv_up: bfloat16 [2, 8192, 512], P('section', 'col', 'row'), may hold values from -0.0625 to 0.0625
- wo_up: bfloat16 [2, 4096, 8192], P('section', 'row', 'col'), may hold values from -0.09375 to 0.09375
Outputs:
- next_down: bfloat16 [2, 1024, 8192], P('section', 'row', 'col')
- next_up: bfloat16 [2, 1024, 8192], P('section', 'row', 'col')
All inputs are finite; a program needn't handle non-finite values.
Results may differ from a plain program's by a relative error of at most 0.0055.
Values may be sent and summed in bfloat16 or wider, within the bound.
No kernel may reach another device: no remote copies, remote signals or barrier semaphores. Data moves between devices by JAX's collectives and lax.ppermute only.
A program may use at most 128 MiB of HBM per device.

v0:
```python
import functools

import jax
import jax.numpy as jnp
from jax import lax
from jax.experimental import pallas as pl
from jax.experimental.pallas import tpu as pltpu
from jax.sharding import PartitionSpec as P

HD = 128
EPSILON = 1e-05
HIDDEN = -1e30
LOG2E = 1.4426950408889634
BF16 = jnp.bfloat16
F32 = jnp.float32


def swapped(value, axis, bit):
    return lax.ppermute(value, axis, [(i, i ^ (1 << bit)) for i in range(lax.axis_size(axis))])


def crossed(value, axis, bits):
    return lax.ppermute(value, axis, [(i, i ^ bits) for i in range(lax.axis_size(axis))])


def from_behind(value, axis, steps):
    count = lax.axis_size(axis)
    return lax.ppermute(value, axis, [(i, (i + steps) % count) for i in range(count)])


def bits_of(axis):
    return lax.axis_size(axis).bit_length() - 1


def my_bit(axis, bit):
    return (lax.axis_index(axis) >> bit) & 1


def pick(value, index, dim):
    return lax.dynamic_index_in_dim(value, index, dim, keepdims=False)


def tie(value, *deps):
    return lax.optimization_barrier((value, deps))[0]


class Chain:
    def __init__(self):
        self.token = None

    def enter(self, *values):
        out = values if self.token is None else tie(values, self.token)
        return out[0] if len(values) == 1 else out

    def leave(self, array):
        self.token = array


def turn(value, cosine, sine):
    return value * cosine + pltpu.roll(value, HD // 2, 1) * sine


def rows_of(keeps, arrivals, inverse, columns):
    parts = [k[:, columns] + a[:, columns].astype(F32) for k, a in zip(keeps, arrivals)]
    return jnp.concatenate(parts, axis=0) * inverse[...]


def kv_kernel(qw, kvw, keep_a, keep_b, arr_a, arr_b, inverse, cosine, sine, out):
    for start in range(0, 2 * kvw, HD):
        columns = slice(qw + start, qw + start + HD)
        value = rows_of((keep_a, keep_b), (arr_a, arr_b), inverse, columns)
        if start < kvw:
            value = turn(value, cosine[...], sine[...])
        out[:, start : start + HD] = value.astype(BF16)


def attention_kernel(
    qw, kvw, count, keep_a, keep_b, arr_a, arr_b, inverse, cosine, sine, q_pos, k_pos, *rest
):
    pairs, (out, keys, values, bias) = rest[:count], rest[count:]
    rows = pairs[0].shape[0]
    for i, pair in enumerate(pairs):
        keys[i * rows : (i + 1) * rows] = pair[:, :kvw]
        values[i * rows : (i + 1) * rows] = pair[:, kvw:]
    bias[...] = jnp.where(q_pos[...] >= k_pos[...], 0.0, HIDDEN)
    group = (qw // HD) // (kvw // HD)
    for head in range(qw // HD):
        columns = slice(head * HD, (head + 1) * HD)
        kv_columns = slice(head // group * HD, (head // group + 1) * HD)
        query = rows_of((keep_a, keep_b), (arr_a, arr_b), inverse, columns)
        query = turn(query, cosine[...], sine[...]).astype(BF16)
        scores = lax.dot_general(
            query, keys[:, kv_columns], (((1,), (1,)), ((), ())), preferred_element_type=F32
        )
        scores = scores + bias[...]
        top = jnp.max(scores, axis=1, keepdims=True)
        probs = jnp.exp2((scores - top) * (LOG2E / HD**0.5))
        total = jnp.sum(probs, axis=1, keepdims=True)
        mixed = jnp.dot(probs.astype(BF16), values[:, kv_columns], preferred_element_type=F32)
        out[:, columns] = (mixed / total).astype(BF16)


def gather(block, axis):
    blocks = {0: block}
    for bit in range(1, bits_of(axis)):
        for o in list(blocks):
            blocks[o | 1 << bit] = swapped(blocks[o], axis, bit)
    return blocks


class Cascade:
    def __init__(self, x, gain, wq, wk, wv, wo):
        self.x, self.gain, self.wo = x, gain, wo
        if wk.shape[1] < HD:
            other_k, other_v = swapped((wk, wv), "row", 0)
            even = lax.axis_index("row") % 2 == 0
            wk = jnp.where(even, jnp.concatenate([wk, other_k], 1), jnp.concatenate([other_k, wk], 1))
            wv = jnp.where(even, jnp.concatenate([wv, other_v], 1), jnp.concatenate([other_v, wv], 1))
        self.qw, self.kvw = wq.shape[1], wk.shape[1]
        self.w = jnp.concatenate([wq, wk, wv], axis=1)
        self.n_row, self.n_col = lax.axis_size("row"), lax.axis_size("col")
        self.sub = x.shape[0] // self.n_col
        self.keep, self.arrived = [], []

    def halves(self, block_list):
        low = my_bit("col", 0)
        blocks = jnp.stack(block_list).reshape(len(block_list), self.n_col // 2, 2, self.sub, -1)
        return pick(blocks, 1 - low, 2), pick(blocks, low, 2)

    def project(self, half):
        scaled = (half.astype(F32) * self.gain).astype(BF16)
        rows = scaled.reshape(-1, scaled.shape[-1])
        out = jnp.dot(rows, self.w, preferred_element_type=F32)
        return out.reshape(half.shape[:-1] + (-1,))

    def halve(self, total, arrived, bit):
        mine = my_bit("col", bit)
        shape = (total.shape[0], -1, 2) + total.shape[2:]
        total, arrived = total.reshape(shape), arrived.reshape(shape)

        def part(which):
            return pick(total, which, 2) + pick(arrived, which, 2).astype(F32)

        return part(mine), part(1 - mine).astype(BF16)

    def flat(self, value):
        return value.reshape(-1, value.shape[-1])

    def kernel_rows(self):
        return [self.flat(v) for v in self.keep] + [self.flat(v) for v in self.arrived]


def whole(body, out_shape, scratch=(), flops=0, exps=0, moved=0):
    return pl.pallas_call(
        body,
        out_shape=out_shape,
        scratch_shapes=list(scratch),
        compiler_params=pltpu.CompilerParams(vmem_limit_bytes=40 * 1024 * 1024),
        cost_estimate=pl.CostEstimate(flops=flops, transcendentals=exps, bytes_accessed=moved),
    )


def on_device(*arrays):
    arrays = [a[0] for a in arrays]
    half = len(arrays) // 2
    d, u = Cascade(*arrays[:half]), Cascade(*arrays[half:])
    n_row, n_col, sub = d.n_row, d.n_col, d.sub
    block = n_col * sub
    features = d.x.shape[1] * n_col
    rows = n_row * sub
    qw, kvw = d.qw, d.kvw
    z, r = lax.axis_index("col"), lax.axis_index("row")
    chain = Chain()

    order = [o for o in range(n_row) if o < 2] + [o for o in range(n_row) if o >= 2]
    starts = (r ^ jnp.array(order, jnp.int32)) * block
    offsets = jnp.arange(sub, dtype=jnp.int32)
    q_pos = (starts[:, None] + z * sub + offsets).astype(F32).reshape(rows, 1)
    owners = (z ^ jnp.arange(n_col, dtype=jnp.int32)) * sub
    k_pos = (owners[:, None, None] + starts[:, None] + offsets).astype(F32).reshape(1, -1)
    width = HD // 2
    inverse_freq = 10000.0 ** (-jnp.arange(width, dtype=F32) / width)
    angles = q_pos * inverse_freq
    cosine = jnp.concatenate([jnp.cos(angles)] * 2, axis=1)
    sine = jnp.sin(angles)
    sine = jnp.concatenate([-sine, sine], axis=1)

    d_blocks = gather(d.x, "row")
    d_blocks[1] = swapped(d.x, "row", 0)

    def send_first(c, group, blocks_):
        send, kept = c.halves(chain.enter(*blocks_))
        product = c.project(send).astype(BF16)
        return product, kept

    def keep_first(c, kept, token):
        return c.project(tie(kept, token))

    def second(c, total, arrived):
        total, arrived = chain.enter(total, arrived)
        kept, product = c.halve(total, arrived, 1)
        arrived = swapped(product, "col", 1)
        chain.leave(product)
        for bit in range(2, bits_of("col")):
            kept, product = c.halve(kept, arrived, bit)
            arrived = swapped(product, "col", bit)
        c.keep.append(kept)
        c.arrived.append(arrived)

    def settle(c):
        c.arrived[-1] = chain.enter(c.arrived[-1])
        chain.leave(c.arrived[-1])

    def take_far(blocks_):
        values = chain.enter(*[blocks_[o] for o in far])
        values = list(values) if len(far) > 1 else [values]
        for o, value in zip(far, values):
            blocks_[o] = value
            blocks_[o | 1] = swapped(value, "row", 0)
        chain.leave(values[-1])
        return values

    far = [o for o in d_blocks if o >= 2]
    far_order = [o for o in order if o >= 2]

    product, kept = send_first(d, 0, [d_blocks[0], d_blocks[1]])
    d_arr_a = swapped(product, "col", 0)
    d_tot_a = keep_first(d, kept, product)
    u_near = swapped(tie(u.x, product), "row", 0)
    chain.leave(d_tot_a)
    squares = jnp.stack([jnp.sum(jnp.square(chain.enter(c.x).astype(F32)), axis=1) for c in (d, u)])
    other = swapped(squares, "col", 0)
    chain.leave(squares)
    u_prod_a, kept = send_first(u, 0, [u.x, u_near])
    u_kept = kept
    chain.leave(u_prod_a)
    squares, other = chain.enter(squares, other)
    squares = squares + other
    other = swapped(squares, "col", 1)
    chain.leave(squares)
    second(d, d_tot_a, d_arr_a)
    u_arr_a = swapped(tie(u_prod_a, chain.token), "col", 0)
    squares, other = chain.enter(squares, other)
    squares = squares + other
    for bit in range(2, bits_of("col")):
        squares = squares + swapped(squares, "col", bit)
    chain.leave(squares)
    sq = gather(squares, "row")

    d_far = take_far(d_blocks)
    u_blocks = gather(tie(u.x, *d_far), "row")
    u_tot_a = u.project(chain.enter(u_kept))
    chain.leave(u_tot_a)
    product, kept = send_first(d, 1, [d_blocks[o] for o in far_order])
    d_arr_b = swapped(product, "col", 0)
    d_tot_b = keep_first(d, kept, product)
    chain.leave(d_tot_b)
    settle(d)
    second(u, u_tot_a, u_arr_a)

    take_far(u_blocks)
    second(d, d_tot_b, d_arr_b)
    for o in list(sq):
        sq[o | 1] = swapped(tie(sq[o], chain.token), "row", 0)
    u_prod_b, kept = send_first(u, 1, [u_blocks[o] for o in far_order])
    u_arr_b = swapped(u_prod_b, "col", 0)
    u_tot_b = keep_first(u, kept, u_prod_b)
    chain.leave(u_tot_b)
    settle(u)

    sums = jnp.stack([sq[o] for o in order])
    sums = pick(sums.reshape(n_row, 2, n_col, sub), z, 2)
    inverse = lax.rsqrt(sums / features + EPSILON).transpose(1, 0, 2).reshape(2, rows, 1)

    def make_pairs(c, scale):
        inputs = chain.enter(*c.kernel_rows())
        pair = whole(
            functools.partial(kv_kernel, qw, kvw),
            jax.ShapeDtypeStruct((rows, 2 * kvw), BF16),
            moved=2 * rows * (qw + 2 * kvw) * 6,
        )(*inputs, scale, cosine, sine)
        chain.leave(pair)
        return inputs, [pair] + [crossed(pair, "col", o) for o in range(1, n_col)]

    def attend(c, inputs, scale, pairs):
        pairs = chain.enter(*pairs)
        keys = rows * n_col
        out = whole(
            functools.partial(attention_kernel, qw, kvw, n_col),
            jax.ShapeDtypeStruct((rows, qw), BF16),
            scratch=[pltpu.VMEM((keys, kvw), BF16), pltpu.VMEM((keys, kvw), BF16), pltpu.VMEM((rows, keys), F32)],
            flops=4 * rows * keys * qw,
            exps=rows * keys * qw // HD,
            moved=rows * qw * 8,
        )(*inputs, scale, cosine, sine, q_pos, k_pos, *pairs)
        chain.leave(out)
        return out

    d_inputs, d_pairs = make_pairs(d, inverse[0])
    second(u, u_tot_b, u_arr_b)
    d_att = attend(d, d_inputs, inverse[0], d_pairs)
    d_got = gather(d_att, "col")
    d_got[1] = swapped(d_att, "col", 0)
    u_inputs, u_pairs = make_pairs(u, inverse[1])

    def out_first(c, pieces):
        pieces = chain.enter(*pieces)
        pieces = pieces if isinstance(pieces, (list, tuple)) else [pieces]
        shaped = jnp.stack([p.reshape(n_row // 2, 2, sub, qw) for p in pieces], axis=2)

        def dot(value):
            out = jnp.dot(value.reshape(-1, qw), c.wo, preferred_element_type=F32)
            return out.reshape(n_row // 2, -1, c.wo.shape[1])

        product = dot(shaped[:, 1]).astype(BF16)
        arrived = swapped(product, "row", 0)
        kept = dot(tie(shaped[:, 0], product))
        chain.leave(kept)
        return kept, arrived

    def out_second(kept, arrived):
        kept, arrived = chain.enter(kept, arrived)
        for bit in range(1, bits_of("row")):
            total = (kept + arrived.astype(F32)).reshape(-1, 2, *kept.shape[1:])
            product = total[:, 1].astype(BF16)
            kept, arrived = total[:, 0], swapped(product, "row", bit)
        chain.leave(product)
        return kept, arrived

    def out_third(c, kept, arrived, which, steps):
        kept, arrived = chain.enter(kept, arrived)
        residual = c.x.reshape(n_col, sub, -1)
        own = jnp.stack([pick(residual, z ^ o, 0) for o in which]).astype(F32)
        total = kept[0] + arrived[0].astype(F32)
        fresh = (own + total.reshape(own.shape)).astype(BF16)
        chain.leave(fresh)
        return from_behind(fresh, "section", steps)

    def finish(c, *sent):
        by_name = {o: piece[i] for names, piece in zip(groups, sent) for i, o in enumerate(names)}
        both = jnp.stack([by_name[o] for o in range(n_col)])
        both = both.reshape((2,) * bits_of("col") + (sub, -1))
        for bit in range(bits_of("col")):
            dim = bits_of("col") - 1 - bit
            both = jnp.where(my_bit("col", bit) == 0, both, jnp.flip(both, dim))
        return both.reshape(c.x.shape)[None]

    def far_pieces(got):
        names = [o for o in got if o >= 2]
        values = chain.enter(*[got[o] for o in names])
        values = list(values) if len(names) > 1 else [values]
        chain.leave(values[-1])
        for o, value in zip(names, values):
            got[o] = value
            got[o | 1] = swapped(value, "col", 0)

    groups = [[0, 1], [o for o in range(2, n_col) if o % 2 == 0], [o for o in range(2, n_col) if o % 2]]

    def first(c, got, i):
        return out_first(c, [got[o] for o in groups[i]])

    far_pieces(d_got)
    u_att = attend(u, u_inputs, inverse[1], u_pairs)
    u_got = gather(u_att, "col")
    u_got[1] = swapped(u_att, "col", 0)
    d_p = first(d, d_got, 0)
    d_p = out_second(*d_p)
    d_m = first(d, d_got, 1)
    d_m = out_second(*d_m)
    d_p = out_third(d, *d_p, groups[0], 1)
    d_q = first(d, d_got, 2)
    u_p = first(u, u_got, 0)
    d_q = out_second(*d_q)
    far_pieces(u_got)
    d_m = out_third(d, *d_m, groups[1], 1)
    u_p = out_second(*u_p)
    u_m = first(u, u_got, 1)
    u_m = out_second(*u_m)
    d_q = out_third(d, *d_q, groups[2], 1)
    u_q = first(u, u_got, 2)
    u_p = out_third(u, *u_p, groups[0], -1)
    u_q = out_second(*u_q)
    u_m = out_third(u, *u_m, groups[1], -1)
    u_q = out_third(u, *u_q, groups[2], -1)
    return finish(d, d_p, d_m, d_q), finish(u, u_p, u_m, u_q)


def solution(mesh):
    tokens = P("section", "row", "col")
    into, out_of = P("section", "col", "row"), P("section", "row", "col")
    one = (tokens, P("section", "col"), into, into, into, out_of)
    return jax.shard_map(
        on_device, mesh=mesh, in_specs=one + one, out_specs=(tokens, tokens), check_vma=False
    )
```

profile of v0, /device:TPU:0, one launch (start us, length us, event | category | flops | bytes accessed | tf_op | source)
XLA Modules:
  0.0 294.7 jit_solution(323983679011132926)
XLA Ops:
  1.1 2.6 collective-permute-start.4
  5.7 4.4 %convolution_convert_fusion.3 = bf16[2,2,64,1280]{3,2,1,0:T(8,128)(2,1)S(1)} fusion(s32[]{:T(128)S(6)} %select_n.81, bf16[1,2,2,64,2048]{4,3,2,1,0:T(8,128)(2,1)} %bitcast.268, bf16[1,2,2,64,2048]{4,3,2,1,0:T(8,128)(2,1)S(1)} %bitcast.292, f32[2048]{0:T(1024)} %bitcast.333, bf16[2048,128]{1,0:T(8,128)(2,1)} %bitcast.317, bf16[2048,128]{1,0:T(8,128)(2,1)} %bitcast.321, ...), kind=kOutput, calls=%fused_computation.31 | convolution fusion | flops 1360330752 | bytes 8003588 | tf_op jit(solution)/shard_map/dot_general | solution.py:133
  10.4 1.6 fusion.46
  11.9 2.2 collective-permute-start.1
  14.8 1.6 convolution_convert_fusion.2
  16.4 13.0 %collective-permute-done.2 = f32[2,256]{1,0:T(2,128)S(1)} collective-permute-done((f32[2,256]{1,0:T(2,128)S(1)}, f32[2,256]{1,0:T(2,128)S(1)}, u32[]{:S(2)}, u32[]{:S(2)}) %collective-permute-start.2) | collective-permute-done | bytes 2080 | tf_op jit(solution)/shard_map/ppermute | solution.py:19
  29.4 2.8 collective-permute-start.5
  32.3 1.6 collective-permute-done.5
  34.0 2.8 collective-permute-start.10
  36.9 1.6 collective-permute-start.9
  38.5 1.6 collective-permute-start.8
  40.1 1.6 fusion.47
  41.7 1.6 convolution_convert_fusion.1
  43.9 1.6 fusion.48
  45.5 6.9 %collective-permute-done.10 = bf16[2,1,64,1280]{3,2,1,0:T(8,128)(2,1)S(1)} collective-permute-done((bf16[2,1,64,1280]{3,2,1,0:T(8,128)(2,1)S(1)}, bf16[2,1,64,1280]{3,2,1,0:T(8,128)(2,1)S(1)}, u32[]{:S(2)}, u32[]{:S(2)}) %collective-permute-start.10) | collective-permute-done | bytes 327712 | tf_op jit(solution)/shard_map/ppermute | solution.py:19
  52.4 7.9 %collective-permute-done.9 = bf16[2,2,64,1280]{3,2,1,0:T(8,128)(2,1)S(1)} collective-permute-done((bf16[2,2,64,1280]{3,2,1,0:T(8,128)(2,1)S(1)}, bf16[2,2,64,1280]{3,2,1,0:T(8,128)(2,1)S(1)}, u32[]{:S(2)}, u32[]{:S(2)}) %collective-permute-start.9) | collective-permute-done | bytes 655392 | tf_op jit(solution)/shard_map/ppermute | solution.py:19
  61.1 2.6 collective-permute-done.8
  63.8 1.5 collective-permute-start.15
  65.3 8.3 %collective-permute-done.7 = bf16[2,2,64,1280]{3,2,1,0:T(8,128)(2,1)S(1)} collective-permute-done((bf16[2,2,64,1280]{3,2,1,0:T(8,128)(2,1)S(1)}, bf16[2,2,64,1280]{3,2,1,0:T(8,128)(2,1)S(1)}, u32[]{:S(2)}, u32[]{:S(2)}) %collective-permute-start.7) | collective-permute-done | bytes 655392 | tf_op jit(solution)/shard_map/ppermute | solution.py:19
  76.1 1.4 collective-permute-start.12
  77.5 1.6 collective-permute-start.11
  79.4 4.8 %convolution_convert_fusion = bf16[2,2,64,1280]{3,2,1,0:T(8,128)(2,1)S(1)} fusion(s32[]{:T(128)S(6)} %select_n.81, bf16[1,2,2,64,2048]{4,3,2,1,0:T(8,128)(2,1)} %bitcast.35, bf16[1,2,2,64,2048]{4,3,2,1,0:T(8,128)(2,1)} %bitcast.36, f32[2048]{0:T(1024)S(1)} %bitcast.339, bf16[2048,128]{1,0:T(8,128)(2,1)} %bitcast.325, bf16[2048,128]{1,0:T(8,128)(2,1)} %bitcast.329, ...), kind=kOutput, calls=%fused_computation.28 | convolution fusion | flops 1360330752 | bytes 8003588 | tf_op jit(solution)/shard_map/dot_general | solution.py:133
  84.2 1.6 collective-permute-start.20
  85.8 1.3 fusion.58
  87.1 1.6 fusion.49
  88.7 13.2 %collective-permute-done.12 = bf16[2,1,64,1280]{3,2,1,0:T(8,128)(2,1)S(1)} collective-permute-done((bf16[2,1,64,1280]{3,2,1,0:T(8,128)(2,1)}, bf16[2,1,64,1280]{3,2,1,0:T(8,128)(2,1)S(1)}, u32[]{:S(2)}, u32[]{:S(2)}) %collective-permute-start.12) | collective-permute-done | bytes 327712 | tf_op jit(solution)/shard_map/ppermute | solution.py:19
  101.9 6.1 %collective-permute-done.11 = bf16[2,1,64,1280]{3,2,1,0:T(8,128)(2,1)S(1)} collective-permute-done((bf16[2,1,64,1280]{3,2,1,0:T(8,128)(2,1)}, bf16[2,1,64,1280]{3,2,1,0:T(8,128)(2,1)S(1)}, u32[]{:S(2)}, u32[]{:S(2)}) %collective-permute-start.11) | collective-permute-done | bytes 327712 | tf_op jit(solution)/shard_map/ppermute | solution.py:19
  108.3 2.8 collective-permute-start.18
  111.1 1.6 collective-permute-start.19
  112.7 4.8 %collective-permute-done.20 = bf16[2,2,64,1280]{3,2,1,0:T(8,128)(2,1)S(1)} collective-permute-done((bf16[2,2,64,1280]{3,2,1,0:T(8,128)(2,1)S(1)}, bf16[2,2,64,1280]{3,2,1,0:T(8,128)(2,1)S(1)}, u32[]{:S(2)}, u32[]{:S(2)}) %collective-permute-start.20) | collective-permute-done | bytes 655392 | tf_op jit(solution)/shard_map/ppermute | solution.py:19
  118.3 3.5 %collective-permute-done.17.rest_1_ = bf16[256,256]{1,0:T(8,128)(2,1)S(1)} collective-permute-done((bf16[256,256]{1,0:T(8,128)(2,1)S(1)}, bf16[256,256]{1,0:T(8,128)(2,1)S(1)}, u32[]{:S(2)}, u32[]{:S(2)}) %collective-permute-start.17) | collective-permute-done | bytes 131104 | tf_op jit(solution)/shard_map/ppermute | solution.py:23
  123.8 4.4 %shard_map.141 = bf16[256,1024]{1,0:T(8,128)(2,1)S(1)} custom-call(f32[128,1280]{1,0:T(8,128)S(1)} %bitcast.248, f32[128,1280]{1,0:T(8,128)S(1)} %bitcast.252, bf16[128,1280]{1,0:T(8,128)(2,1)S(1)} %bitcast.258, bf16[128,1280]{1,0:T(8,128)(2,1)S(1)} %bitcast.262, f32[256,1]{1,0:T(8,128)S(1)} %squeeze.166.inverse, f32[256,128]{1,0:T(8,128)S(1)} %pad_maximum_fusion.4.cosine, ...), custom_call_target="tpu_custom_call" | custom-call | flops 1073741824 | bytes 2097152 | tf_op jit(solution)/shard_map/pallas_call | solution.py:288
  128.2 2.7 collective-permute-start.26
  131.2 1.7 collective-permute-start.21
  133.1 34.4 %collective-permute-done.22 = bf16[2,1,64,1280]{3,2,1,0:T(8,128)(2,1)S(1)} collective-permute-done((bf16[2,1,64,1280]{3,2,1,0:T(8,128)(2,1)}, bf16[2,1,64,1280]{3,2,1,0:T(8,128)(2,1)S(1)}, u32[]{:S(2)}, u32[]{:S(2)}) %collective-permute-start.22) | collective-permute-done | bytes 327712 | tf_op jit(solution)/shard_map/ppermute | solution.py:19
  168.8 3.3 %collective-permute-start.24 = (bf16[256,256]{1,0:T(8,128)(2,1)S(1)}, bf16[256,256]{1,0:T(8,128)(2,1)S(1)}, u32[]{:S(2)}, u32[]{:S(2)}) collective-permute-start(bf16[256,256]{1,0:T(8,128)(2,1)S(1)} %shard_map.142.rest_0_), channel_id=1, source_target_pairs={{0,2},{1,3},{2,0},{3,1},{4,6},{5,7},{6,4},{7,5},{8,10},{9,11},{10,... | collective-permute-start | bytes 393224 | tf_op jit(solution)/shard_map/ppermute | solution.py:23
  173.1 1.9 collective-permute-done.23.rest_1_
  175.0 6.7 %collective-permute-done.24.rest_2_ = bf16[256,256]{1,0:T(8,128)(2,1)S(1)} collective-permute-done((bf16[256,256]{1,0:T(8,128)(2,1)S(1)}, bf16[256,256]{1,0:T(8,128)(2,1)S(1)}, u32[]{:S(2)}, u32[]{:S(2)}) %collective-permute-start.24) | collective-permute-done | bytes 131104 | tf_op jit(solution)/shard_map/ppermute | solution.py:23
  183.6 4.5 %shard_map.143 = bf16[256,1024]{1,0:T(8,128)(2,1)S(1)} custom-call(f32[128,1280]{1,0:T(8,128)S(1)} %bitcast.250, f32[128,1280]{1,0:T(8,128)S(1)} %bitcast.254, bf16[128,1280]{1,0:T(8,128)(2,1)S(1)} %bitcast.260, bf16[128,1280]{1,0:T(8,128)(2,1)S(1)} %bitcast.264, f32[256,1]{1,0:T(8,128)S(1)} %squeeze.167.inverse, f32[256,128]{1,0:T(8,128)S(1)} %pad_maximum_fusion.4.cosine, ...), custom_call_target="tpu_custom_call" | custom-call | flops 1073741824 | bytes 2097152 | tf_op jit(solution)/shard_map/pallas_call | solution.py:288
  188.1 1.9 pad_maximum_fusion.3
  190.1 12.0 %fusion.24 = bf16[2,128,2048]{2,1,0:T(8,128)(2,1)} fusion(bf16[2,128,1024]{2,1,0:T(8,128)(2,1)S(1)} %bitcast.303, bf16[1,1024,2048]{2,1,0:T(8,128)(2,1)S(1)} %copy-done.9), kind=kOutput, calls=%fused_computation.26 | convolution fusion | flops 1074266112 | bytes 5767168 | tf_op jit(solution)/shard_map/dot_general | solution.py:312
  202.2 2.0 collective-permute-start.33
  204.3 3.0 %collective-permute-start.32 = (bf16[256,1024]{1,0:T(8,128)(2,1)S(1)}, bf16[256,1024]{1,0:T(8,128)(2,1)S(1)}, u32[]{:S(2)}, u32[]{:S(2)}) collective-permute-start(bf16[256,1024]{1,0:T(8,128)(2,1)S(1)} %shard_map.143), channel_id=1, source_target_pairs={{0,2},{1,3},{2,0},{3,1},{4,6},{5,7},{6,4},{7,5},{8,10},{9,11},{10,... | collective-permute-start | bytes 1572872 | tf_op jit(solution)/shard_map/ppermute | solution.py:19
  207.3 3.5 %fusion.20 = f32[2,128,2048]{2,1,0:T(8,128)S(1)} fusion(bf16[2,128,1024]{2,1,0:T(8,128)(2,1)S(1)} %bitcast.285, bf16[1,1024,2048]{2,1,0:T(8,128)(2,1)} %param.18), kind=kOutput, calls=%fused_computation.22 | convolution fusion | flops 1073741824 | bytes 6815744 | tf_op jit(solution)/shard_map/dot_general | solution.py:312
  210.8 1.7 add_bitcast_fusion.1
  213.3 1.7 fusion.30
  215.9 1.6 collective-permute-start.28
  220.2 10.7 %collective-permute-done.28 = bf16[1,128,2048]{2,1,0:T(8,128)(2,1)S(1)} collective-permute-done((bf16[1,128,2048]{2,1,0:T(8,128)(2,1)S(1)}, bf16[1,128,2048]{2,1,0:T(8,128)(2,1)S(1)}, u32[]{:S(2)}, u32[]{:S(2)}) %collective-permute-start.28) | collective-permute-done | bytes 524320 | tf_op jit(solution)/shard_map/ppermute | solution.py:19
  231.1 1.6 collective-permute-start.30
  234.3 5.2 %collective-permute-done.35 = bf16[256,1024]{1,0:T(8,128)(2,1)S(1)} collective-permute-done((bf16[256,1024]{1,0:T(8,128)(2,1)S(1)}, bf16[256,1024]{1,0:T(8,128)(2,1)S(1)}, u32[]{:S(2)}, u32[]{:S(2)}) %collective-permute-start.35) | collective-permute-done | bytes 524320 | tf_op jit(solution)/shard_map/ppermute | solution.py:19
  239.6 1.3 fusion.27
  242.5 1.6 collective-permute-start.37
  244.2 1.6 collective-permute-start.36
  249.7 1.6 collective-permute-done.37
  251.3 1.9 collective-permute-start.44
  253.3 4.8 %collective-permute-done.42 = bf16[256,1024]{1,0:T(8,128)(2,1)S(1)} collective-permute-done((bf16[256,1024]{1,0:T(8,128)(2,1)S(1)}, bf16[256,1024]{1,0:T(8,128)(2,1)S(1)}, u32[]{:S(2)}, u32[]{:S(2)}) %collective-permute-start.42) | collective-permute-done | bytes 524320 | tf_op jit(solution)/shard_map/ppermute | solution.py:19
  259.7 4.1 %collective-permute-done.41 = bf16[1,128,2048]{2,1,0:T(8,128)(2,1)S(1)} collective-permute-done((bf16[1,128,2048]{2,1,0:T(8,128)(2,1)S(1)}, bf16[1,128,2048]{2,1,0:T(8,128)(2,1)S(1)}, u32[]{:S(2)}, u32[]{:S(2)}) %collective-permute-start.41) | collective-permute-done | bytes 524320 | tf_op jit(solution)/shard_map/ppermute | solution.py:19
  264.8 1.4 collective-permute-start.43
  266.2 6.8 %collective-permute-done.40 = bf16[1,64,2048]{2,1,0:T(8,128)(2,1)S(1)} collective-permute-done((bf16[1,64,2048]{2,1,0:T(8,128)(2,1)S(1)}, bf16[1,64,2048]{2,1,0:T(8,128)(2,1)S(1)}, u32[]{:S(2)}, u32[]{:S(2)}) %collective-permute-start.40) | collective-permute-done | bytes 262176 | tf_op jit(solution)/shard_map/ppermute | solution.py:28
  274.4 1.6 collective-permute-start.46
  276.0 4.0 %collective-permute-done.47 = bf16[1,64,2048]{2,1,0:T(8,128)(2,1)S(1)} collective-permute-done((bf16[1,64,2048]{2,1,0:T(8,128)(2,1)S(1)}, bf16[1,64,2048]{2,1,0:T(8,128)(2,1)S(1)}, u32[]{:S(2)}, u32[]{:S(2)}) %collective-permute-start.47) | collective-permute-done | bytes 262176 | tf_op jit(solution)/shard_map/ppermute | solution.py:19
  282.0 2.2 collective-permute-done.43
  284.3 5.6 %collective-permute-done.46 = bf16[1,64,2048]{2,1,0:T(8,128)(2,1)S(1)} collective-permute-done((bf16[1,64,2048]{2,1,0:T(8,128)(2,1)S(1)}, bf16[1,64,2048]{2,1,0:T(8,128)(2,1)S(1)}, u32[]{:S(2)}, u32[]{:S(2)}) %collective-permute-start.46) | collective-permute-done | bytes 262176 | tf_op jit(solution)/shard_map/ppermute | solution.py:28
  289.9 3.1 %collective-permute-done.48 = bf16[1,64,2048]{2,1,0:T(8,128)(2,1)S(1)} collective-permute-done((bf16[1,64,2048]{2,1,0:T(8,128)(2,1)S(1)}, bf16[1,64,2048]{2,1,0:T(8,128)(2,1)S(1)}, u32[]{:S(2)}, u32[]{:S(2)}) %collective-permute-start.48) | collective-permute-done | bytes 262176 | tf_op jit(solution)/shard_map/ppermute | solution.py:28
  (191 shorter events, 35.4 us)
Async XLA Ops:
  0.6 3.8 %collective-permute-start = (bf16[256,2048]{1,0:T(8,128)(2,1)}, bf16[256,2048]{1,0:T(8,128)(2,1)S(1)}, u32[]{:S(2)}, u32[]{:S(2)}) collective-permute-start(bf16[256,2048]{1,0:T(8,128)(2,1)} %bitcast.265), channel_id=1, source_target_pairs={{0,4},{4,0},{8,12},{12,8},{1,5},{5,1},{9,13},{13,9},{2,6},{6,2},{1... | collective-permute-start | bytes 3145736 | tf_op jit(solution)/shard_map/ppermute | solution.py:19
  1.1 32.8 %collective-permute-start.4 = (bf16[256,2048]{1,0:T(8,128)(2,1)}, bf16[256,2048]{1,0:T(8,128)(2,1)S(1)}, u32[]{:S(2)}, u32[]{:S(2)}) collective-permute-start(bf16[256,2048]{1,0:T(8,128)(2,1)} %bitcast.266), channel_id=1, source_target_pairs={{0,8},{4,12},{8,0},{12,4},{1,9},{5,13},{9,1},{13,5},{2,10},{6,14},... | collective-permute-start | bytes 3145736 | tf_op jit(solution)/shard_map/ppermute | solution.py:19
  5.6 4.7 %copy-start.17 = (bf16[1,2048,1024]{2,1,0:T(8,128)(2,1)S(1)}, bf16[1,2048,1024]{2,1,0:T(8,128)(2,1)}, u32[]{:S(2)}) copy-start(bf16[1,2048,1024]{2,1,0:T(8,128)(2,1)} %param.15) | copy-start | bytes 12582916
  10.1 4.7 %copy-start.18 = (bf16[1,2048,1024]{2,1,0:T(8,128)(2,1)S(1)}, bf16[1,2048,1024]{2,1,0:T(8,128)(2,1)}, u32[]{:S(2)}) copy-start(bf16[1,2048,1024]{2,1,0:T(8,128)(2,1)} %param.21) | copy-start | bytes 12582916
  10.1 4.7 %copy-start.22 = (bf16[1,2048,128]{2,1,0:T(8,128)(2,1)S(1)}, bf16[1,2048,128]{2,1,0:T(8,128)(2,1)}, u32[]{:S(2)}) copy-start(bf16[1,2048,128]{2,1,0:T(8,128)(2,1)} %param.23) | copy-start | bytes 1572868
  10.1 4.7 %collective-permute-start.3 = (bf16[256,2048]{1,0:T(8,128)(2,1)S(1)}, bf16[256,2048]{1,0:T(8,128)(2,1)S(1)}, u32[]{:S(2)}, u32[]{:S(2)}) collective-permute-start(bf16[256,2048]{1,0:T(8,128)(2,1)S(1)} %bitcast.273), channel_id=1, source_target_pairs={{0,4},{4,0},{8,12},{12,8},{1,5},{5,1},{9,13},{13,9},{2,6},{6,2},{1... | collective-permute-start | bytes 3145736 | tf_op jit(solution)/shard_map/ppermute | solution.py:19
  11.9 20.2 %collective-permute-start.1 = (bf16[2,2,64,1280]{3,2,1,0:T(8,128)(2,1)S(1)}, bf16[2,2,64,1280]{3,2,1,0:T(8,128)(2,1)S(1)}, u32[]{:S(2)}, u32[]{:S(2)}) collective-permute-start(bf16[2,2,64,1280]{3,2,1,0:T(8,128)(2,1)S(1)} %convolution_convert_fusion.3), channel_id=1, source_target_pairs={{0,1},{1,0},{2,3},{3,2},{4,5},{5,4},{6,7},{7,6},{8,9},{9,8},{10,11... | collective-permute-start | bytes 1966088 | tf_op jit(solution)/shard_map/ppermute | solution.py:19
  14.7 14.7 %collective-permute-start.2 = (f32[2,256]{1,0:T(2,128)S(1)}, f32[2,256]{1,0:T(2,128)S(1)}, u32[]{:S(2)}, u32[]{:S(2)}) collective-permute-start(f32[2,256]{1,0:T(2,128)S(1)} %pad_maximum_fusion.6), channel_id=1, source_target_pairs={{0,1},{1,0},{2,3},{3,2},{4,5},{5,4},{6,7},{7,6},{8,9},{9,8},{10,11... | collective-permute-start | bytes 6152 | tf_op jit(solution)/shard_map/ppermute | solution.py:19
  29.4 4.5 %collective-permute-start.5 = (f32[2,256]{1,0:T(2,128)S(1)}, f32[2,256]{1,0:T(2,128)S(1)}, u32[]{:S(2)}, u32[]{:S(2)}) collective-permute-start(f32[2,256]{1,0:T(2,128)S(1)} %add.248), channel_id=1, source_target_pairs={{0,2},{1,3},{2,0},{3,1},{4,6},{5,7},{6,4},{7,5},{8,10},{9,11},{10,... | collective-permute-start | bytes 6152 | tf_op jit(solution)/shard_map/ppermute | solution.py:19
  33.9 7.8 %collective-permute-start.6 = (bf16[256,2048]{1,0:T(8,128)(2,1)S(1)}, bf16[256,2048]{1,0:T(8,128)(2,1)S(1)}, u32[]{:S(2)}, u32[]{:S(2)}) collective-permute-start(bf16[256,2048]{1,0:T(8,128)(2,1)S(1)} %collective-permute-done.4), channel_id=1, source_target_pairs={{0,4},{4,0},{8,12},{12,8},{1,5},{5,1},{9,13},{13,9},{2,6},{6,2},{1... | collective-permute-start | bytes 3145736 | tf_op jit(solution)/shard_map/ppermute | solution.py:19
  34.0 18.3 %collective-permute-start.10 = (bf16[2,1,64,1280]{3,2,1,0:T(8,128)(2,1)S(1)}, bf16[2,1,64,1280]{3,2,1,0:T(8,128)(2,1)S(1)}, u32[]{:S(2)}, u32[]{:S(2)}) collective-permute-start(bf16[2,1,64,1280]{3,2,1,0:T(8,128)(2,1)S(1)} %get-tuple-element.188), channel_id=1, source_target_pairs={{0,2},{1,3},{2,0},{3,1},{4,6},{5,7},{6,4},{7,5},{8,10},{9,11},{10,... | collective-permute-start | bytes 983048 | tf_op jit(solution)/shard_map/ppermute | solution.py:19
  36.9 23.4 %collective-permute-start.9 = (bf16[2,2,64,1280]{3,2,1,0:T(8,128)(2,1)S(1)}, bf16[2,2,64,1280]{3,2,1,0:T(8,128)(2,1)S(1)}, u32[]{:S(2)}, u32[]{:S(2)}) collective-permute-start(bf16[2,2,64,1280]{3,2,1,0:T(8,128)(2,1)S(1)} %convolution_convert_fusion.2), channel_id=1, source_target_pairs={{0,1},{1,0},{2,3},{3,2},{4,5},{5,4},{6,7},{7,6},{8,9},{9,8},{10,11... | collective-permute-start | bytes 1966088 | tf_op jit(solution)/shard_map/ppermute | solution.py:19
  38.5 25.2 %collective-permute-start.8 = (bf16[256,2048]{1,0:T(8,128)(2,1)S(1)}, bf16[256,2048]{1,0:T(8,128)(2,1)}, u32[]{:S(2)}, u32[]{:S(2)}) collective-permute-start(bf16[256,2048]{1,0:T(8,128)(2,1)S(1)} %bitcast.277), channel_id=1, source_target_pairs={{0,8},{4,12},{8,0},{12,4},{1,9},{5,13},{9,1},{13,5},{2,10},{6,14},... | collective-permute-start | bytes 3145736 | tf_op jit(solution)/shard_map/ppermute | solution.py:19
  43.4 30.2 %collective-permute-start.7 = (bf16[2,2,64,1280]{3,2,1,0:T(8,128)(2,1)S(1)}, bf16[2,2,64,1280]{3,2,1,0:T(8,128)(2,1)S(1)}, u32[]{:S(2)}, u32[]{:S(2)}) collective-permute-start(bf16[2,2,64,1280]{3,2,1,0:T(8,128)(2,1)S(1)} %convolution_convert_fusion.1), channel_id=1, source_target_pairs={{0,1},{1,0},{2,3},{3,2},{4,5},{5,4},{6,7},{7,6},{8,9},{9,8},{10,11... | collective-permute-start | bytes 1966088 | tf_op jit(solution)/shard_map/ppermute | solution.py:19
  52.3 55.7 %copy-start = (bf16[2,1,64,1280]{3,2,1,0:T(8,128)(2,1)}, bf16[2,1,64,1280]{3,2,1,0:T(8,128)(2,1)S(1)}, u32[]{:S(2)}) copy-start(bf16[2,1,64,1280]{3,2,1,0:T(8,128)(2,1)S(1)} %collective-permute-done.10) | copy-start | bytes 983044
  63.7 15.7 %collective-permute-start.13 = (bf16[256,2048]{1,0:T(8,128)(2,1)}, bf16[256,2048]{1,0:T(8,128)(2,1)}, u32[]{:S(2)}, u32[]{:S(2)}) collective-permute-start(bf16[256,2048]{1,0:T(8,128)(2,1)} %collective-permute-done.8), channel_id=1, source_target_pairs={{0,4},{4,0},{8,12},{12,8},{1,5},{5,1},{9,13},{13,9},{2,6},{6,2},{1... | collective-permute-start | bytes 3145736 | tf_op jit(solution)/shard_map/ppermute | solution.py:19
  63.8 10.6 %collective-permute-start.15 = (f32[2,256]{1,0:T(2,128)S(1)}, f32[2,256]{1,0:T(2,128)S(1)}, u32[]{:S(2)}, u32[]{:S(2)}) collective-permute-start(f32[2,256]{1,0:T(2,128)S(1)} %add.253), channel_id=1, source_target_pairs={{0,8},{4,12},{8,0},{12,4},{1,9},{5,13},{9,1},{13,5},{2,10},{6,14},... | collective-permute-start | bytes 6152 | tf_op jit(solution)/shard_map/ppermute | solution.py:19
  74.4 4.6 %collective-permute-start.14 = (f32[2,256]{1,0:T(2,128)S(1)}, f32[2,256]{1,0:T(2,128)S(1)}, u32[]{:S(2)}, u32[]{:S(2)}) collective-permute-start(f32[2,256]{1,0:T(2,128)S(1)} %add.253), channel_id=1, source_target_pairs={{0,4},{4,0},{8,12},{12,8},{1,5},{5,1},{9,13},{13,9},{2,6},{6,2},{1... | collective-permute-start | bytes 6152 | tf_op jit(solution)/shard_map/ppermute | solution.py:19
  74.4 4.7 %collective-permute-start.16 = (f32[2,256]{1,0:T(2,128)S(1)}, f32[2,256]{1,0:T(2,128)S(1)}, u32[]{:S(2)}, u32[]{:S(2)}) collective-permute-start(f32[2,256]{1,0:T(2,128)S(1)} %collective-permute-done.15), channel_id=1, source_target_pairs={{0,4},{4,0},{8,12},{12,8},{1,5},{5,1},{9,13},{13,9},{2,6},{6,2},{1... | collective-permute-start | bytes 6152 | tf_op jit(solution)/shard_map/ppermute | solution.py:19
  76.1 25.8 %collective-permute-start.12 = (bf16[2,1,64,1280]{3,2,1,0:T(8,128)(2,1)}, bf16[2,1,64,1280]{3,2,1,0:T(8,128)(2,1)S(1)}, u32[]{:S(2)}, u32[]{:S(2)}) collective-permute-start(bf16[2,1,64,1280]{3,2,1,0:T(8,128)(2,1)} %get-tuple-element.185), channel_id=1, source_target_pairs={{0,2},{1,3},{2,0},{3,1},{4,6},{5,7},{6,4},{7,5},{8,10},{9,11},{10,... | collective-permute-start | bytes 983048 | tf_op jit(solution)/shard_map/ppermute | solution.py:19
  77.5 30.5 %collective-permute-start.11 = (bf16[2,1,64,1280]{3,2,1,0:T(8,128)(2,1)}, bf16[2,1,64,1280]{3,2,1,0:T(8,128)(2,1)S(1)}, u32[]{:S(2)}, u32[]{:S(2)}) collective-permute-start(bf16[2,1,64,1280]{3,2,1,0:T(8,128)(2,1)} %get-tuple-element.186), channel_id=1, source_target_pairs={{0,2},{1,3},{2,0},{3,1},{4,6},{5,7},{6,4},{7,5},{8,10},{9,11},{10,... | collective-permute-start | bytes 983048 | tf_op jit(solution)/shard_map/ppermute | solution.py:19
  79.4 7.7 %copy-start.19 = (bf16[1,2048,1024]{2,1,0:T(8,128)(2,1)S(1)}, bf16[1,2048,1024]{2,1,0:T(8,128)(2,1)}, u32[]{:S(2)}) copy-start(bf16[1,2048,1024]{2,1,0:T(8,128)(2,1)} %param.21) | copy-start | bytes 12582916
  79.4 7.7 %copy-start.23 = (bf16[1,2048,128]{2,1,0:T(8,128)(2,1)S(1)}, bf16[1,2048,128]{2,1,0:T(8,128)(2,1)}, u32[]{:S(2)}) copy-start(bf16[1,2048,128]{2,1,0:T(8,128)(2,1)} %param.23) | copy-start | bytes 1572868
  79.4 7.7 %copy-start.25 = (bf16[1,2048,128]{2,1,0:T(8,128)(2,1)S(1)}, bf16[1,2048,128]{2,1,0:T(8,128)(2,1)}, u32[]{:S(2)}) copy-start(bf16[1,2048,128]{2,1,0:T(8,128)(2,1)} %param.22) | copy-start | bytes 1572868
  84.2 33.2 %collective-permute-start.20 = (bf16[2,2,64,1280]{3,2,1,0:T(8,128)(2,1)S(1)}, bf16[2,2,64,1280]{3,2,1,0:T(8,128)(2,1)S(1)}, u32[]{:S(2)}, u32[]{:S(2)}) collective-permute-start(bf16[2,2,64,1280]{3,2,1,0:T(8,128)(2,1)S(1)} %convolution_convert_fusion), channel_id=1, source_target_pairs={{0,1},{1,0},{2,3},{3,2},{4,5},{5,4},{6,7},{7,6},{8,9},{9,8},{10,11... | collective-permute-start | bytes 1966088 | tf_op jit(solution)/shard_map/ppermute | solution.py:19
  88.7 33.1 %copy-start.7 = (f32[256,1]{1,0:T(8,128)S(1)}, f32[256,1]{1,0:T(8,128)}, u32[]{:S(2)}) copy-start(f32[256,1]{1,0:T(8,128)} %convert_element_type.437.q_pos) | copy-start | bytes 3076
  101.9 10.7 %copy-start.2 = (bf16[2,1,64,1280]{3,2,1,0:T(8,128)(2,1)}, bf16[2,1,64,1280]{3,2,1,0:T(8,128)(2,1)S(1)}, u32[]{:S(2)}) copy-start(bf16[2,1,64,1280]{3,2,1,0:T(8,128)(2,1)S(1)} %collective-permute-done.12) | copy-start | bytes 983044
  108.0 13.8 %copy-start.5 = (bf16[2,1,64,1280]{3,2,1,0:T(8,128)(2,1)}, bf16[2,1,64,1280]{3,2,1,0:T(8,128)(2,1)S(1)}, u32[]{:S(2)}) copy-start(bf16[2,1,64,1280]{3,2,1,0:T(8,128)(2,1)S(1)} %collective-permute-done.11) | copy-start | bytes 983044
  108.2 13.6 %collective-permute-start.17 = (bf16[256,256]{1,0:T(8,128)(2,1)S(1)}, bf16[256,256]{1,0:T(8,128)(2,1)S(1)}, u32[]{:S(2)}, u32[]{:S(2)}) collective-permute-start(bf16[256,256]{1,0:T(8,128)(2,1)S(1)} %shard_map.140.rest_0_), channel_id=1, source_target_pairs={{0,1},{1,0},{2,3},{3,2},{4,5},{5,4},{6,7},{7,6},{8,9},{9,8},{10,11... | collective-permute-start | bytes 393224 | tf_op jit(solution)/shard_map/ppermute | solution.py:23
  108.3 13.5 %collective-permute-start.18 = (bf16[256,256]{1,0:T(8,128)(2,1)S(1)}, bf16[256,256]{1,0:T(8,128)(2,1)S(1)}, u32[]{:S(2)}, u32[]{:S(2)}) collective-permute-start(bf16[256,256]{1,0:T(8,128)(2,1)S(1)} %shard_map.140.rest_0_), channel_id=1, source_target_pairs={{0,2},{1,3},{2,0},{3,1},{4,6},{5,7},{6,4},{7,5},{8,10},{9,11},{10,... | collective-permute-start | bytes 393224 | tf_op jit(solution)/shard_map/ppermute | solution.py:23
  111.1 10.7 %collective-permute-start.19 = (bf16[256,256]{1,0:T(8,128)(2,1)S(1)}, bf16[256,256]{1,0:T(8,128)(2,1)S(1)}, u32[]{:S(2)}, u32[]{:S(2)}) collective-permute-start(bf16[256,256]{1,0:T(8,128)(2,1)S(1)} %shard_map.140.rest_0_), channel_id=1, source_target_pairs={{0,3},{1,2},{2,1},{3,0},{4,7},{5,6},{6,5},{7,4},{8,11},{9,10},{10,... | collective-permute-start | bytes 393224 | tf_op jit(solution)/shard_map/ppermute | solution.py:23
  128.2 44.9 %collective-permute-start.26 = (bf16[256,1024]{1,0:T(8,128)(2,1)S(1)}, bf16[256,1024]{1,0:T(8,128)(2,1)}, u32[]{:S(2)}, u32[]{:S(2)}) collective-permute-start(bf16[256,1024]{1,0:T(8,128)(2,1)S(1)} %shard_map.141), channel_id=1, source_target_pairs={{0,2},{1,3},{2,0},{3,1},{4,6},{5,7},{6,4},{7,5},{8,10},{9,11},{10,... | collective-permute-start | bytes 1572872 | tf_op jit(solution)/shard_map/ppermute | solution.py:19
  131.0 36.5 %collective-permute-start.22 = (bf16[2,1,64,1280]{3,2,1,0:T(8,128)(2,1)}, bf16[2,1,64,1280]{3,2,1,0:T(8,128)(2,1)S(1)}, u32[]{:S(2)}, u32[]{:S(2)}) collective-permute-start(bf16[2,1,64,1280]{3,2,1,0:T(8,128)(2,1)} %get-tuple-element.183), channel_id=1, source_target_pairs={{0,2},{1,3},{2,0},{3,1},{4,6},{5,7},{6,4},{7,5},{8,10},{9,11},{10,... | collective-permute-start | bytes 983048 | tf_op jit(solution)/shard_map/ppermute | solution.py:19
  131.2 56.8 %collective-permute-start.21 = (bf16[256,1024]{1,0:T(8,128)(2,1)S(1)}, bf16[256,1024]{1,0:T(8,128)(2,1)}, u32[]{:S(2)}, u32[]{:S(2)}) collective-permute-start(bf16[256,1024]{1,0:T(8,128)(2,1)S(1)} %shard_map.141), channel_id=1, source_target_pairs={{0,1},{1,0},{2,3},{3,2},{4,5},{5,4},{6,7},{7,6},{8,9},{9,8},{10,11... | collective-permute-start | bytes 1572872 | tf_op jit(solution)/shard_map/ppermute | solution.py:19
  168.7 6.3 %collective-permute-start.23 = (bf16[256,256]{1,0:T(8,128)(2,1)S(1)}, bf16[256,256]{1,0:T(8,128)(2,1)S(1)}, u32[]{:S(2)}, u32[]{:S(2)}) collective-permute-start(bf16[256,256]{1,0:T(8,128)(2,1)S(1)} %shard_map.142.rest_0_), channel_id=1, source_target_pairs={{0,1},{1,0},{2,3},{3,2},{4,5},{5,4},{6,7},{7,6},{8,9},{9,8},{10,11... | collective-permute-start | bytes 393224 | tf_op jit(solution)/shard_map/ppermute | solution.py:23
  168.8 12.9 %collective-permute-start.24 = (bf16[256,256]{1,0:T(8,128)(2,1)S(1)}, bf16[256,256]{1,0:T(8,128)(2,1)S(1)}, u32[]{:S(2)}, u32[]{:S(2)}) collective-permute-start(bf16[256,256]{1,0:T(8,128)(2,1)S(1)} %shard_map.142.rest_0_), channel_id=1, source_target_pairs={{0,2},{1,3},{2,0},{3,1},{4,6},{5,7},{6,4},{7,5},{8,10},{9,11},{10,... | collective-permute-start | bytes 393224 | tf_op jit(solution)/shard_map/ppermute | solution.py:23
  172.1 9.6 %collective-permute-start.25 = (bf16[256,256]{1,0:T(8,128)(2,1)S(1)}, bf16[256,256]{1,0:T(8,128)(2,1)S(1)}, u32[]{:S(2)}, u32[]{:S(2)}) collective-permute-start(bf16[256,256]{1,0:T(8,128)(2,1)S(1)} %shard_map.142.rest_0_), channel_id=1, source_target_pairs={{0,3},{1,2},{2,1},{3,0},{4,7},{5,6},{6,5},{7,4},{8,11},{9,10},{10,... | collective-permute-start | bytes 393224 | tf_op jit(solution)/shard_map/ppermute | solution.py:23
  183.6 6.4 %copy-start.9 = (bf16[1,1024,2048]{2,1,0:T(8,128)(2,1)S(1)}, bf16[1,1024,2048]{2,1,0:T(8,128)(2,1)}, u32[]{:S(2)}) copy-start(bf16[1,1024,2048]{2,1,0:T(8,128)(2,1)} %param.18) | copy-start | bytes 12582916
  190.0 12.1 %copy-start.13 = (bf16[1,256,2048]{2,1,0:T(8,128)(2,1)S(1)}, bf16[1,256,2048]{2,1,0:T(8,128)(2,1)}, u32[]{:S(2)}) copy-start(bf16[1,256,2048]{2,1,0:T(8,128)(2,1)} %param.13) | copy-start | bytes 3145732
  190.0 12.1 %copy-start.15 = (bf16[1,256,2048]{2,1,0:T(8,128)(2,1)S(1)}, bf16[1,256,2048]{2,1,0:T(8,128)(2,1)}, u32[]{:S(2)}) copy-start(bf16[1,256,2048]{2,1,0:T(8,128)(2,1)} %param.19) | copy-start | bytes 3145732
  190.1 17.2 %copy-start.16 = (bf16[2,2,64,1024]{3,2,0,1:T(8,128)(2,1)S(1)}, bf16[2,2,64,1024]{3,2,0,1:T(8,128)(2,1)}, u32[]{:S(2)}) copy-start(bf16[2,2,64,1024]{3,2,0,1:T(8,128)(2,1)} %get-tuple-element.143) | copy-start | bytes 1572868
  202.1 8.7 %collective-permute-start.27 = (bf16[2,128,2048]{2,1,0:T(8,128)(2,1)}, bf16[2,128,2048]{2,1,0:T(8,128)(2,1)}, u32[]{:S(2)}, u32[]{:S(2)}) collective-permute-start(bf16[2,128,2048]{2,1,0:T(8,128)(2,1)} %fusion.24), channel_id=1, source_target_pairs={{0,4},{4,0},{8,12},{12,8},{1,5},{5,1},{9,13},{13,9},{2,6},{6,2},{1... | collective-permute-start | bytes 3145736 | tf_op jit(solution)/shard_map/ppermute | solution.py:19
  202.2 30.5 %collective-permute-start.33 = (bf16[256,1024]{1,0:T(8,128)(2,1)}, bf16[256,1024]{1,0:T(8,128)(2,1)S(1)}, u32[]{:S(2)}, u32[]{:S(2)}) collective-permute-start(bf16[256,1024]{1,0:T(8,128)(2,1)} %collective-permute-done.26), channel_id=1, source_target_pairs={{0,1},{1,0},{2,3},{3,2},{4,5},{5,4},{6,7},{7,6},{8,9},{9,8},{10,11... | collective-permute-start | bytes 1572872 | tf_op jit(solution)/shard_map/ppermute | solution.py:19
  204.2 35.3 %collective-permute-start.35 = (bf16[256,1024]{1,0:T(8,128)(2,1)S(1)}, bf16[256,1024]{1,0:T(8,128)(2,1)S(1)}, u32[]{:S(2)}, u32[]{:S(2)}) collective-permute-start(bf16[256,1024]{1,0:T(8,128)(2,1)S(1)} %shard_map.143), channel_id=1, source_target_pairs={{0,1},{1,0},{2,3},{3,2},{4,5},{5,4},{6,7},{7,6},{8,9},{9,8},{10,11... | collective-permute-start | bytes 1572872 | tf_op jit(solution)/shard_map/ppermute | solution.py:19
  204.3 39.8 %collective-permute-start.32 = (bf16[256,1024]{1,0:T(8,128)(2,1)S(1)}, bf16[256,1024]{1,0:T(8,128)(2,1)S(1)}, u32[]{:S(2)}, u32[]{:S(2)}) collective-permute-start(bf16[256,1024]{1,0:T(8,128)(2,1)S(1)} %shard_map.143), channel_id=1, source_target_pairs={{0,2},{1,3},{2,0},{3,1},{4,6},{5,7},{6,4},{7,5},{8,10},{9,11},{10,... | collective-permute-start | bytes 1572872 | tf_op jit(solution)/shard_map/ppermute | solution.py:19
  215.9 14.9 %collective-permute-start.28 = (bf16[1,128,2048]{2,1,0:T(8,128)(2,1)S(1)}, bf16[1,128,2048]{2,1,0:T(8,128)(2,1)S(1)}, u32[]{:S(2)}, u32[]{:S(2)}) collective-permute-start(bf16[1,128,2048]{2,1,0:T(8,128)(2,1)S(1)} %fusion.86), channel_id=1, source_target_pairs={{0,8},{4,12},{8,0},{12,4},{1,9},{5,13},{9,1},{13,5},{2,10},{6,14},... | collective-permute-start | bytes 1572872 | tf_op jit(solution)/shard_map/ppermute | solution.py:19
  217.5 1.9 collective-permute-start.29
  219.6 24.5 %collective-permute-start.31 = (bf16[1,64,2048]{2,1,0:T(8,128)(2,1)S(1)}, bf16[1,64,2048]{2,1,0:T(8,128)(2,1)S(1)}, u32[]{:S(2)}, u32[]{:S(2)}) collective-permute-start(bf16[1,64,2048]{2,1,0:T(8,128)(2,1)S(1)} %fusion.88), channel_id=1, source_target_pairs={{0,8},{4,12},{8,0},{12,4},{1,9},{5,13},{9,1},{13,5},{2,10},{6,14},... | collective-permute-start | bytes 786440 | tf_op jit(solution)/shard_map/ppermute | solution.py:19
  231.1 33.7 %collective-permute-start.30 = (bf16[2,64,2048]{2,1,0:T(8,128)(2,1)S(1)}, bf16[2,64,2048]{2,1,0:T(8,128)(2,1)S(1)}, u32[]{:S(2)}, u32[]{:S(2)}) collective-permute-start(bf16[2,64,2048]{2,1,0:T(8,128)(2,1)S(1)} %add_convert_fusion.1), channel_id=1, source_target_pairs={{0,16},{16,0},{1,17},{17,1},{2,18},{18,2},{3,19},{19,3},{4,20},{20... | collective-permute-start | bytes 1572872 | tf_op jit(solution)/shard_map/ppermute | solution.py:28
  233.4 8.9 %collective-permute-start.34 = (bf16[2,64,2048]{2,1,0:T(8,128)(2,1)S(1)}, bf16[2,64,2048]{2,1,0:T(8,128)(2,1)S(1)}, u32[]{:S(2)}, u32[]{:S(2)}) collective-permute-start(bf16[2,64,2048]{2,1,0:T(8,128)(2,1)S(1)} %fusion.33), channel_id=1, source_target_pairs={{0,4},{4,0},{8,12},{12,8},{1,5},{5,1},{9,13},{13,9},{2,6},{6,2},{1... | collective-permute-start | bytes 1572872 | tf_op jit(solution)/shard_map/ppermute | solution.py:19
  233.5 6.1 %copy-start.11 = (bf16[1,1024,2048]{2,1,0:T(8,128)(2,1)S(1)}, bf16[1,1024,2048]{2,1,0:T(8,128)(2,1)}, u32[]{:S(2)}) copy-start(bf16[1,1024,2048]{2,1,0:T(8,128)(2,1)} %param.24) | copy-start | bytes 12582916
  240.9 4.9 %collective-permute-start.38 = (bf16[2,128,2048]{2,1,0:T(8,128)(2,1)S(1)}, bf16[2,128,2048]{2,1,0:T(8,128)(2,1)S(1)}, u32[]{:S(2)}, u32[]{:S(2)}) collective-permute-start(bf16[2,128,2048]{2,1,0:T(8,128)(2,1)S(1)} %fusion.27), channel_id=1, source_target_pairs={{0,4},{4,0},{8,12},{12,8},{1,5},{5,1},{9,13},{13,9},{2,6},{6,2},{1... | collective-permute-start | bytes 3145736 | tf_op jit(solution)/shard_map/ppermute | solution.py:19
  242.5 8.8 %collective-permute-start.37 = (bf16[1,64,2048]{2,1,0:T(8,128)(2,1)S(1)}, bf16[1,64,2048]{2,1,0:T(8,128)(2,1)S(1)}, u32[]{:S(2)}, u32[]{:S(2)}) collective-permute-start(bf16[1,64,2048]{2,1,0:T(8,128)(2,1)S(1)} %fusion.89), channel_id=1, source_target_pairs={{0,8},{4,12},{8,0},{12,4},{1,9},{5,13},{9,1},{13,5},{2,10},{6,14},... | collective-permute-start | bytes 786440 | tf_op jit(solution)/shard_map/ppermute | solution.py:19
  244.1 14.0 %collective-permute-start.42 = (bf16[256,1024]{1,0:T(8,128)(2,1)S(1)}, bf16[256,1024]{1,0:T(8,128)(2,1)S(1)}, u32[]{:S(2)}, u32[]{:S(2)}) collective-permute-start(bf16[256,1024]{1,0:T(8,128)(2,1)S(1)} %collective-permute-done.32), channel_id=1, source_target_pairs={{0,1},{1,0},{2,3},{3,2},{4,5},{5,4},{6,7},{7,6},{8,9},{9,8},{10,11... | collective-permute-start | bytes 1572872 | tf_op jit(solution)/shard_map/ppermute | solution.py:19
  244.2 22.0 %collective-permute-start.36 = (bf16[1,64,2048]{2,1,0:T(8,128)(2,1)S(1)}, bf16[1,64,2048]{2,1,0:T(8,128)(2,1)S(1)}, u32[]{:S(2)}, u32[]{:S(2)}) collective-permute-start(bf16[1,64,2048]{2,1,0:T(8,128)(2,1)S(1)} %add_convert_fusion.9), channel_id=1, source_target_pairs={{0,16},{16,0},{1,17},{17,1},{2,18},{18,2},{3,19},{19,3},{4,20},{20... | collective-permute-start | bytes 786440 | tf_op jit(solution)/shard_map/ppermute | solution.py:28
  247.0 2.0 collective-permute-start.39
  249.0 14.8 %collective-permute-start.41 = (bf16[1,128,2048]{2,1,0:T(8,128)(2,1)S(1)}, bf16[1,128,2048]{2,1,0:T(8,128)(2,1)S(1)}, u32[]{:S(2)}, u32[]{:S(2)}) collective-permute-start(bf16[1,128,2048]{2,1,0:T(8,128)(2,1)S(1)} %fusion.87), channel_id=1, source_target_pairs={{0,8},{4,12},{8,0},{12,4},{1,9},{5,13},{9,1},{13,5},{2,10},{6,14},... | collective-permute-start | bytes 1572872 | tf_op jit(solution)/shard_map/ppermute | solution.py:19
  251.3 23.0 %collective-permute-start.44 = (bf16[1,64,2048]{2,1,0:T(8,128)(2,1)S(1)}, bf16[1,64,2048]{2,1,0:T(8,128)(2,1)S(1)}, u32[]{:S(2)}, u32[]{:S(2)}) collective-permute-start(bf16[1,64,2048]{2,1,0:T(8,128)(2,1)S(1)} %fusion.90), channel_id=1, source_target_pairs={{0,8},{4,12},{8,0},{12,4},{1,9},{5,13},{9,1},{13,5},{2,10},{6,14},... | collective-permute-start | bytes 786440 | tf_op jit(solution)/shard_map/ppermute | solution.py:19
  258.9 14.5 %collective-permute-start.45 = (bf16[2,64,2048]{2,1,0:T(8,128)(2,1)S(1)}, bf16[2,64,2048]{2,1,0:T(8,128)(2,1)S(1)}, u32[]{:S(2)}, u32[]{:S(2)}) collective-permute-start(bf16[2,64,2048]{2,1,0:T(8,128)(2,1)S(1)} %fusion.39), channel_id=1, source_target_pairs={{0,4},{4,0},{8,12},{12,8},{1,5},{5,1},{9,13},{13,9},{2,6},{6,2},{1... | collective-permute-start | bytes 1572872 | tf_op jit(solution)/shard_map/ppermute | solution.py:19
  263.8 9.2 %collective-permute-start.40 = (bf16[1,64,2048]{2,1,0:T(8,128)(2,1)S(1)}, bf16[1,64,2048]{2,1,0:T(8,128)(2,1)S(1)}, u32[]{:S(2)}, u32[]{:S(2)}) collective-permute-start(bf16[1,64,2048]{2,1,0:T(8,128)(2,1)S(1)} %add_convert_fusion.8), channel_id=1, source_target_pairs={{0,16},{16,0},{1,17},{17,1},{2,18},{18,2},{3,19},{19,3},{4,20},{20... | collective-permute-start | bytes 786440 | tf_op jit(solution)/shard_map/ppermute | solution.py:28
  264.8 19.5 %collective-permute-start.43 = (bf16[2,64,2048]{2,1,0:T(8,128)(2,1)S(1)}, bf16[2,64,2048]{2,1,0:T(8,128)(2,1)S(1)}, u32[]{:S(2)}, u32[]{:S(2)}) collective-permute-start(bf16[2,64,2048]{2,1,0:T(8,128)(2,1)S(1)} %add_convert_fusion), channel_id=1, source_target_pairs={{0,16},{16,0},{1,17},{17,1},{2,18},{18,2},{3,19},{19,3},{4,20},{20... | collective-permute-start | bytes 1572872 | tf_op jit(solution)/shard_map/ppermute | solution.py:28
  273.6 6.4 %collective-permute-start.47 = (bf16[1,64,2048]{2,1,0:T(8,128)(2,1)S(1)}, bf16[1,64,2048]{2,1,0:T(8,128)(2,1)S(1)}, u32[]{:S(2)}, u32[]{:S(2)}) collective-permute-start(bf16[1,64,2048]{2,1,0:T(8,128)(2,1)S(1)} %fusion.91), channel_id=1, source_target_pairs={{0,8},{4,12},{8,0},{12,4},{1,9},{5,13},{9,1},{13,5},{2,10},{6,14},... | collective-permute-start | bytes 786440 | tf_op jit(solution)/shard_map/ppermute | solution.py:19
  274.4 15.5 %collective-permute-start.46 = (bf16[1,64,2048]{2,1,0:T(8,128)(2,1)S(1)}, bf16[1,64,2048]{2,1,0:T(8,128)(2,1)S(1)}, u32[]{:S(2)}, u32[]{:S(2)}) collective-permute-start(bf16[1,64,2048]{2,1,0:T(8,128)(2,1)S(1)} %add_convert_fusion.7), channel_id=1, source_target_pairs={{0,16},{16,0},{1,17},{17,1},{2,18},{18,2},{3,19},{19,3},{4,20},{20... | collective-permute-start | bytes 786440 | tf_op jit(solution)/shard_map/ppermute | solution.py:28
  280.1 12.9 %collective-permute-start.48 = (bf16[1,64,2048]{2,1,0:T(8,128)(2,1)S(1)}, bf16[1,64,2048]{2,1,0:T(8,128)(2,1)S(1)}, u32[]{:S(2)}, u32[]{:S(2)}) collective-permute-start(bf16[1,64,2048]{2,1,0:T(8,128)(2,1)S(1)} %add_convert_fusion.6), channel_id=1, source_target_pairs={{0,16},{16,0},{1,17},{17,1},{2,18},{18,2},{3,19},{19,3},{4,20},{20... | collective-permute-start | bytes 786440 | tf_op jit(solution)/shard_map/ppermute | solution.py:28
  (13 other events, 39.7 us)
where the time goes:
time: 299 us; the launch traced here: 295 us
  waiting for transfers between devices  161 us (54%)
  starting transfers between devices  54.6 us (18%)
  matrix products  43.4 us (15%)
  other arithmetic  15.5 us (5%)
  Pallas kernels  9.3 us (3%)
  local copies, waits for them, and re-layouts  8.98 us (3%)
    ppermute x37, waiting for transfers between devices, swapped(): lax.ppermute(value, axis, [(i, i ^ 1 << bit) for i in range(lax.axis_size...  131 us
    ppermute x37, starting transfers between devices, swapped(): lax.ppermute(value, axis, [(i, i ^ 1 << bit) for i in range(lax.axis_size...  38.2 us
    dot_general x12, matrix products, dot(): out = jnp.dot(value.reshape(-1, qw), c.wo, preferred_element_type=F32)  24.7 us
    dot_general x8, matrix products, project(): out = jnp.dot(rows, self.w, preferred_element_type=F32)  18.6 us
    ppermute x6, waiting for transfers between devices, from_behind(): lax.ppermute(value, axis, [(i, (i + steps) % count) for i in range(count)])  17.8 us
    ppermute x6, waiting for transfers between devices, crossed(): lax.ppermute(value, axis, [(i, i ^ bits) for i in range(lax.axis_size(axi...  12.1 us
    pallas_call x2, Pallas kernels, attend(): whole(functools.partial(attention_kernel, qw, kvw, n_col), jax.ShapeDtype...  8.9 us
    ppermute x6, starting transfers between devices, crossed(): lax.ppermute(value, axis, [(i, i ^ bits) for i in range(lax.axis_size(axi...  8.9 us
  transfers between devices with their start and end apart: 49, of which 25 were waited for; matrix products, arithmetic and copies ran while one was open for 16% of the time, Pallas kernels for 2%

commit v1 on v0

--- a/solution.py
+++ b/solution.py
@@ -297,11 +297,16 @@
         return out
 
     d_inputs, d_pairs = make_pairs(d, inverse[0])
+    d_pairs = list(chain.enter(*d_pairs))
+    chain.leave(d_pairs[-1])
     second(u, u_tot_b, u_arr_b)
     d_att = attend(d, d_inputs, inverse[0], d_pairs)
     d_got = gather(d_att, "col")
     d_got[1] = swapped(d_att, "col", 0)
     u_inputs, u_pairs = make_pairs(u, inverse[1])
+    u_att = attend(u, u_inputs, inverse[1], u_pairs)
+    u_got = gather(u_att, "col")
+    u_got[1] = swapped(u_att, "col", 0)
 
     def out_first(c, pieces):
         pieces = chain.enter(*pieces)
@@ -359,28 +364,25 @@
     def first(c, got, i):
         return out_first(c, [got[o] for o in groups[i]])
 
+    d_p = first(d, d_got, 0)
     far_pieces(d_got)
-    u_att = attend(u, u_inputs, inverse[1], u_pairs)
-    u_got = gather(u_att, "col")
-    u_got[1] = swapped(u_att, "col", 0)
-    d_p = first(d, d_got, 0)
     d_p = out_second(*d_p)
     d_m = first(d, d_got, 1)
     d_m = out_second(*d_m)
+    u_p = first(u, u_got, 0)
+    far_pieces(u_got)
     d_p = out_third(d, *d_p, groups[0], 1)
+    u_p = out_second(*u_p)
+    d_m = out_third(d, *d_m, groups[1], 1)
     d_q = first(d, d_got, 2)
-    u_p = first(u, u_got, 0)
+    u_m = first(u, u_got, 1)
     d_q = out_second(*d_q)
-    far_pieces(u_got)
-    d_m = out_third(d, *d_m, groups[1], 1)
-    u_p = out_second(*u_p)
-    u_m = first(u, u_got, 1)
     u_m = out_second(*u_m)
+    u_p = out_third(u, *u_p, groups[0], -1)
     d_q = out_third(d, *d_q, groups[2], 1)
+    u_m = out_third(u, *u_m, groups[1], -1)
     u_q = first(u, u_got, 2)
-    u_p = out_third(u, *u_p, groups[0], -1)
     u_q = out_second(*u_q)
-    u_m = out_third(u, *u_m, groups[1], -1)
     u_q = out_third(u, *u_q, groups[2], -1)
     return finish(d, d_p, d_m, d_q), finish(u, u_p, u_m, u_q)
 

time: 299 us -> 299 us (level)
  waiting for transfers between devices: 161 us -> 148 us
  local copies, waits for them, and re-layouts: 8.98 us -> 15.8 us
  Pallas kernels: 9.3 us -> 12.3 us
    ppermute x37, waiting for transfers between devices: 131 us -> 109 us  [swapped(): lax.ppermute(value, axis, [(i, i ^ 1 << bit) for i in range(lax.axis_size...]
    ppermute x6, waiting for transfers between devices: 12.1 us -> 24.1 us  [crossed(): lax.ppermute(value, axis, [(i, i ^ bits) for i in range(lax.axis_size(axi...]
    unnamed x56 -> x72, local copies, waits for them, and re-layouts: 5.58 us -> 9.94 us
  transfers between devices with their start and end apart: 49 -> 49, of which waited for: 25 -> 22; matrix products, arithmetic and copies ran while one was open for 16% -> 17% of each run, Pallas kernels for 2% -> 4%
where the time goes in v1:
time: 299 us; the launch traced here: 295 us
  waiting for transfers between devices  148 us (49%)
  starting transfers between devices  54.5 us (18%)
  matrix products  45.4 us (15%)
  other arithmetic  16.8 us (6%)
  local copies, waits for them, and re-layouts  15.8 us (5%)
  Pallas kernels  12.3 us (4%)
    ppermute x37, waiting for transfers between devices, swapped(): lax.ppermute(value, axis, [(i, i ^ 1 << bit) for i in range(lax.axis_size...  109 us
    ppermute x37, starting transfers between devices, swapped(): lax.ppermute(value, axis, [(i, i ^ 1 << bit) for i in range(lax.axis_size...  37.2 us
    dot_general x12, matrix products, dot(): out = jnp.dot(value.reshape(-1, qw), c.wo, preferred_element_type=F32)  24.8 us
    ppermute x6, waiting for transfers between devices, crossed(): lax.ppermute(value, axis, [(i, i ^ bits) for i in range(lax.axis_size(axi...  24.1 us
    dot_general x8, matrix products, project(): out = jnp.dot(rows, self.w, preferred_element_type=F32)  20.5 us
    ppermute x6, waiting for transfers between devices, from_behind(): lax.ppermute(value, axis, [(i, (i + steps) % count) for i in range(count)])  15.1 us
    pallas_call x2, Pallas kernels, attend(): whole(functools.partial(attention_kernel, qw, kvw, n_col), jax.ShapeDtype...  11 us
    unnamed x72, local copies, waits for them, and re-layouts  9.94 us
  transfers between devices with their start and end apart: 49, of which 22 were waited for; matrix products, arithmetic and copies ran while one was open for 17% of the time, Pallas kernels for 4%

profile of v1, /device:TPU:0, one launch (start us, length us, event | category | flops | bytes accessed | tf_op | source)
XLA Modules:
  0.0 294.8 jit_solution(14025933427673711326)
XLA Ops:
  1.1 2.6 collective-permute-start.4
  5.1 4.4 %convolution_convert_fusion.3 = bf16[2,2,64,1280]{3,2,1,0:T(8,128)(2,1)S(1)} fusion(s32[]{:T(128)S(6)} %select_n.81, bf16[1,2,2,64,2048]{4,3,2,1,0:T(8,128)(2,1)} %bitcast.266, bf16[1,2,2,64,2048]{4,3,2,1,0:T(8,128)(2,1)S(1)} %bitcast.290, f32[2048]{0:T(1024)} %bitcast.331, bf16[2048,128]{1,0:T(8,128)(2,1)} %bitcast.315, bf16[2048,128]{1,0:T(8,128)(2,1)} %bitcast.319, ...), kind=kOutput, calls=%fused_computation.31 | convolution fusion | flops 1360330752 | bytes 8003588 | tf_op jit(solution)/shard_map/dot_general | solution.py:133
  9.5 2.8 collective-permute-start.1
  12.4 1.6 fusion.46
  15.0 1.6 convolution_convert_fusion.2
  16.6 10.7 %collective-permute-done.2 = f32[2,256]{1,0:T(2,128)S(1)} collective-permute-done((f32[2,256]{1,0:T(2,128)S(1)}, f32[2,256]{1,0:T(2,128)S(1)}, u32[]{:S(2)}, u32[]{:S(2)}) %collective-permute-start.2) | collective-permute-done | bytes 2080 | tf_op jit(solution)/shard_map/ppermute | solution.py:19
  27.3 2.8 collective-permute-start.5
  30.2 1.6 collective-permute-done.5
  32.4 2.8 collective-permute-start.10
  35.2 1.6 collective-permute-start.9
  36.9 1.6 collective-permute-start.8
  38.4 1.6 fusion.47
  40.0 1.6 convolution_convert_fusion.1
  42.2 1.6 fusion.48
  43.8 6.9 %collective-permute-done.10 = bf16[2,1,64,1280]{3,2,1,0:T(8,128)(2,1)S(1)} collective-permute-done((bf16[2,1,64,1280]{3,2,1,0:T(8,128)(2,1)S(1)}, bf16[2,1,64,1280]{3,2,1,0:T(8,128)(2,1)S(1)}, u32[]{:S(2)}, u32[]{:S(2)}) %collective-permute-start.10) | collective-permute-done | bytes 327712 | tf_op jit(solution)/shard_map/ppermute | solution.py:19
  50.7 7.9 %collective-permute-done.9 = bf16[2,2,64,1280]{3,2,1,0:T(8,128)(2,1)S(1)} collective-permute-done((bf16[2,2,64,1280]{3,2,1,0:T(8,128)(2,1)S(1)}, bf16[2,2,64,1280]{3,2,1,0:T(8,128)(2,1)S(1)}, u32[]{:S(2)}, u32[]{:S(2)}) %collective-permute-start.9) | collective-permute-done | bytes 655392 | tf_op jit(solution)/shard_map/ppermute | solution.py:19
  59.5 2.6 collective-permute-done.8
  62.2 1.5 collective-permute-start.15
  63.7 8.2 %collective-permute-done.7 = bf16[2,2,64,1280]{3,2,1,0:T(8,128)(2,1)S(1)} collective-permute-done((bf16[2,2,64,1280]{3,2,1,0:T(8,128)(2,1)S(1)}, bf16[2,2,64,1280]{3,2,1,0:T(8,128)(2,1)S(1)}, u32[]{:S(2)}, u32[]{:S(2)}) %collective-permute-start.7) | collective-permute-done | bytes 655392 | tf_op jit(solution)/shard_map/ppermute | solution.py:19
  74.3 1.4 collective-permute-start.12
  75.7 1.6 collective-permute-start.11
  77.7 1.3 fusion.58
  79.0 5.6 %convolution_convert_fusion = bf16[2,2,64,1280]{3,2,1,0:T(8,128)(2,1)} fusion(s32[]{:T(128)S(6)} %select_n.81, bf16[1,2,2,64,2048]{4,3,2,1,0:T(8,128)(2,1)} %bitcast.35, bf16[1,2,2,64,2048]{4,3,2,1,0:T(8,128)(2,1)} %bitcast.36, f32[2048]{0:T(1024)S(1)} %bitcast.337, bf16[2048,128]{1,0:T(8,128)(2,1)} %bitcast.323, bf16[2048,128]{1,0:T(8,128)(2,1)} %bitcast.327, ...), kind=kOutput, calls=%fused_computation.28 | convolution fusion | flops 1360330752 | bytes 8003588 | tf_op jit(solution)/shard_map/dot_general | solution.py:133
  84.6 1.5 collective-permute-start.20
  86.1 2.6 fusion.49
  88.8 11.4 %collective-permute-done.12 = bf16[2,1,64,1280]{3,2,1,0:T(8,128)(2,1)S(1)} collective-permute-done((bf16[2,1,64,1280]{3,2,1,0:T(8,128)(2,1)}, bf16[2,1,64,1280]{3,2,1,0:T(8,128)(2,1)S(1)}, u32[]{:S(2)}, u32[]{:S(2)}) %collective-permute-start.12) | collective-permute-done | bytes 327712 | tf_op jit(solution)/shard_map/ppermute | solution.py:19
  100.2 6.1 %collective-permute-done.11 = bf16[2,1,64,1280]{3,2,1,0:T(8,128)(2,1)S(1)} collective-permute-done((bf16[2,1,64,1280]{3,2,1,0:T(8,128)(2,1)}, bf16[2,1,64,1280]{3,2,1,0:T(8,128)(2,1)S(1)}, u32[]{:S(2)}, u32[]{:S(2)}) %collective-permute-start.11) | collective-permute-done | bytes 327712 | tf_op jit(solution)/shard_map/ppermute | solution.py:19
  106.5 2.8 collective-permute-start.18
  109.4 1.6 collective-permute-start.19
  111.1 11.3 %collective-permute-done.17.rest_1_ = bf16[256,256]{1,0:T(8,128)(2,1)S(1)} collective-permute-done((bf16[256,256]{1,0:T(8,128)(2,1)S(1)}, bf16[256,256]{1,0:T(8,128)(2,1)S(1)}, u32[]{:S(2)}, u32[]{:S(2)}) %collective-permute-start.17) | collective-permute-done | bytes 131104 | tf_op jit(solution)/shard_map/ppermute | solution.py:23
  123.7 2.3 convert_add_fusion.2
  126.0 1.5 collective-permute-start.22
  133.1 5.4 %shard_map.141 = bf16[256,1024]{1,0:T(8,128)(2,1)S(1)} custom-call(f32[128,1280]{1,0:T(8,128)S(1)} %bitcast.248, f32[128,1280]{1,0:T(8,128)S(1)} %bitcast.252, bf16[128,1280]{1,0:T(8,128)(2,1)S(1)} %bitcast.258, bf16[128,1280]{1,0:T(8,128)(2,1)S(1)} %bitcast.262, f32[256,1]{1,0:T(8,128)S(1)} %squeeze.166.inverse, f32[256,128]{1,0:T(8,128)S(1)} %pad_maximum_fusion.4.cosine, ...), custom_call_target="tpu_custom_call" | custom-call | flops 1073741824 | bytes 2097152 | tf_op jit(solution)/shard_map/pallas_call | solution.py:288
  138.5 2.6 collective-permute-start.21
  141.2 1.4 collective-permute-done.22
  144.8 2.9 collective-permute-start.24
  147.7 1.5 collective-permute-start.25
  149.2 12.9 %collective-permute-done.23.rest_1_ = bf16[256,256]{1,0:T(8,128)(2,1)S(1)} collective-permute-done((bf16[256,256]{1,0:T(8,128)(2,1)S(1)}, bf16[256,256]{1,0:T(8,128)(2,1)S(1)}, u32[]{:S(2)}, u32[]{:S(2)}) %collective-permute-start.23) | collective-permute-done | bytes 131104 | tf_op jit(solution)/shard_map/ppermute | solution.py:23
  163.9 5.6 %shard_map.143 = bf16[256,1024]{1,0:T(8,128)(2,1)S(1)} custom-call(f32[128,1280]{1,0:T(8,128)S(1)} %bitcast.250, f32[128,1280]{1,0:T(8,128)S(1)} %bitcast.254, bf16[128,1280]{1,0:T(8,128)(2,1)S(1)} %bitcast.260, bf16[128,1280]{1,0:T(8,128)(2,1)} %bitcast.44.arr_b, f32[256,1]{1,0:T(8,128)S(1)} %squeeze.167.inverse, f32[256,128]{1,0:T(8,128)S(1)} %pad_maximum_fusion.4.cosine, ...), custom_call_target="tpu_custom_call" | custom-call | flops 1073741824 | bytes 2097152 | tf_op jit(solution)/shard_map/pallas_call | solution.py:288
  169.5 1.9 pad_maximum_fusion.3
  171.5 12.1 %fusion.24 = bf16[2,128,2048]{2,1,0:T(8,128)(2,1)} fusion(bf16[2,128,1024]{2,1,0:T(8,128)(2,1)S(1)} %bitcast.301, bf16[1,1024,2048]{2,1,0:T(8,128)(2,1)S(1)} %copy-done.15), kind=kOutput, calls=%fused_computation.26 | convolution fusion | flops 1074266112 | bytes 5767168 | tf_op jit(solution)/shard_map/dot_general | solution.py:317
  185.6 2.5 collective-permute-start.30
  189.2 3.5 %fusion.20 = f32[2,128,2048]{2,1,0:T(8,128)S(1)} fusion(bf16[2,128,1024]{2,1,0:T(8,128)(2,1)S(1)} %bitcast.283, bf16[1,1024,2048]{2,1,0:T(8,128)(2,1)} %param.18), kind=kOutput, calls=%fused_computation.22 | convolution fusion | flops 1073741824 | bytes 6815744 | tf_op jit(solution)/shard_map/dot_general | solution.py:317
  192.7 18.3 %collective-permute-done.27 = bf16[256,1024]{1,0:T(8,128)(2,1)} collective-permute-done((bf16[256,1024]{1,0:T(8,128)(2,1)S(1)}, bf16[256,1024]{1,0:T(8,128)(2,1)}, u32[]{:S(2)}, u32[]{:S(2)}) %collective-permute-start.27) | collective-permute-done | bytes 524320 | tf_op jit(solution)/shard_map/ppermute | solution.py:19
  211.0 1.6 add_bitcast_fusion.1
  213.6 1.7 fusion.30
  215.3 1.6 collective-permute-start.28
  219.8 1.3 fusion.27
  221.7 1.3 fusion.8
  223.0 10.2 %collective-permute-done.29 = bf16[256,1024]{1,0:T(8,128)(2,1)S(1)} collective-permute-done((bf16[256,1024]{1,0:T(8,128)(2,1)S(1)}, bf16[256,1024]{1,0:T(8,128)(2,1)S(1)}, u32[]{:S(2)}, u32[]{:S(2)}) %collective-permute-start.29) | collective-permute-done | bytes 524320 | tf_op jit(solution)/shard_map/ppermute | solution.py:19
  233.5 1.6 collective-permute-start.32
  238.7 1.6 collective-permute-start.39
  241.3 1.6 collective-permute-start.35
  243.9 9.6 %collective-permute-done.39 = bf16[1,128,2048]{2,1,0:T(8,128)(2,1)S(1)} collective-permute-done((bf16[1,128,2048]{2,1,0:T(8,128)(2,1)S(1)}, bf16[1,128,2048]{2,1,0:T(8,128)(2,1)S(1)}, u32[]{:S(2)}, u32[]{:S(2)}) %collective-permute-start.39) | collective-permute-done | bytes 524320 | tf_op jit(solution)/shard_map/ppermute | solution.py:19
  253.5 1.5 collective-permute-start.43
  255.3 3.8 %collective-permute-done.38 = bf16[1,64,2048]{2,1,0:T(8,128)(2,1)S(1)} collective-permute-done((bf16[1,64,2048]{2,1,0:T(8,128)(2,1)S(1)}, bf16[1,64,2048]{2,1,0:T(8,128)(2,1)S(1)}, u32[]{:S(2)}, u32[]{:S(2)}) %collective-permute-start.38) | collective-permute-done | bytes 262176 | tf_op jit(solution)/shard_map/ppermute | solution.py:19
  259.1 1.5 collective-permute-start.42
  260.8 3.6 %collective-permute-done.43 = bf16[1,64,2048]{2,1,0:T(8,128)(2,1)S(1)} collective-permute-done((bf16[1,64,2048]{2,1,0:T(8,128)(2,1)S(1)}, bf16[1,64,2048]{2,1,0:T(8,128)(2,1)S(1)}, u32[]{:S(2)}, u32[]{:S(2)}) %collective-permute-start.43) | collective-permute-done | bytes 262176 | tf_op jit(solution)/shard_map/ppermute | solution.py:19
  264.3 1.6 collective-permute-start.41
  268.1 11.5 %collective-permute-done.41 = bf16[1,64,2048]{2,1,0:T(8,128)(2,1)S(1)} collective-permute-done((bf16[1,64,2048]{2,1,0:T(8,128)(2,1)S(1)}, bf16[1,64,2048]{2,1,0:T(8,128)(2,1)S(1)}, u32[]{:S(2)}, u32[]{:S(2)}) %collective-permute-start.41) | collective-permute-done | bytes 262176 | tf_op jit(solution)/shard_map/ppermute | solution.py:28
  280.1 1.6 collective-permute-start.47
  281.7 4.8 %collective-permute-done.47 = bf16[1,64,2048]{2,1,0:T(8,128)(2,1)S(1)} collective-permute-done((bf16[1,64,2048]{2,1,0:T(8,128)(2,1)S(1)}, bf16[1,64,2048]{2,1,0:T(8,128)(2,1)S(1)}, u32[]{:S(2)}, u32[]{:S(2)}) %collective-permute-start.47) | collective-permute-done | bytes 262176 | tf_op jit(solution)/shard_map/ppermute | solution.py:19
  286.6 1.6 collective-permute-start.48
  289.5 3.6 %collective-permute-done.48 = bf16[1,64,2048]{2,1,0:T(8,128)(2,1)S(1)} collective-permute-done((bf16[1,64,2048]{2,1,0:T(8,128)(2,1)S(1)}, bf16[1,64,2048]{2,1,0:T(8,128)(2,1)S(1)}, u32[]{:S(2)}, u32[]{:S(2)}) %collective-permute-start.48) | collective-permute-done | bytes 262176 | tf_op jit(solution)/shard_map/ppermute | solution.py:28
  (207 shorter events, 39.1 us)
Async XLA Ops:
  0.6 3.3 %collective-permute-start = (bf16[256,2048]{1,0:T(8,128)(2,1)}, bf16[256,2048]{1,0:T(8,128)(2,1)S(1)}, u32[]{:S(2)}, u32[]{:S(2)}) collective-permute-start(bf16[256,2048]{1,0:T(8,128)(2,1)} %bitcast.263), channel_id=1, source_target_pairs={{0,4},{4,0},{8,12},{12,8},{1,5},{5,1},{9,13},{13,9},{2,6},{6,2},{1... | collective-permute-start | bytes 3145736 | tf_op jit(solution)/shard_map/ppermute | solution.py:19
  1.1 30.7 %collective-permute-start.4 = (bf16[256,2048]{1,0:T(8,128)(2,1)}, bf16[256,2048]{1,0:T(8,128)(2,1)S(1)}, u32[]{:S(2)}, u32[]{:S(2)}) collective-permute-start(bf16[256,2048]{1,0:T(8,128)(2,1)} %bitcast.264), channel_id=1, source_target_pairs={{0,8},{4,12},{8,0},{12,4},{1,9},{5,13},{9,1},{13,5},{2,10},{6,14},... | collective-permute-start | bytes 3145736 | tf_op jit(solution)/shard_map/ppermute | solution.py:19
  5.1 7.3 %copy-start.25 = (bf16[1,2048,1024]{2,1,0:T(8,128)(2,1)S(1)}, bf16[1,2048,1024]{2,1,0:T(8,128)(2,1)}, u32[]{:S(2)}) copy-start(bf16[1,2048,1024]{2,1,0:T(8,128)(2,1)} %param.15) | copy-start | bytes 12582916
  5.1 7.3 %copy-start.28 = (bf16[1,2048,128]{2,1,0:T(8,128)(2,1)S(1)}, bf16[1,2048,128]{2,1,0:T(8,128)(2,1)}, u32[]{:S(2)}) copy-start(bf16[1,2048,128]{2,1,0:T(8,128)(2,1)} %param.17) | copy-start | bytes 1572868
  5.1 7.3 %copy-start.29 = (bf16[1,2048,128]{2,1,0:T(8,128)(2,1)S(1)}, bf16[1,2048,128]{2,1,0:T(8,128)(2,1)}, u32[]{:S(2)}) copy-start(bf16[1,2048,128]{2,1,0:T(8,128)(2,1)} %param.16) | copy-start | bytes 1572868
  5.1 7.3 %copy-start.34 = (f32[1,2048]{1,0:T(1,128)S(1)}, f32[1,2048]{1,0:T(1,128)}, u32[]{:S(2)}) copy-start(f32[1,2048]{1,0:T(1,128)} %param.14) | copy-start | bytes 24580
  9.5 20.6 %collective-permute-start.1 = (bf16[2,2,64,1280]{3,2,1,0:T(8,128)(2,1)S(1)}, bf16[2,2,64,1280]{3,2,1,0:T(8,128)(2,1)S(1)}, u32[]{:S(2)}, u32[]{:S(2)}) collective-permute-start(bf16[2,2,64,1280]{3,2,1,0:T(8,128)(2,1)S(1)} %convolution_convert_fusion.3), channel_id=1, source_target_pairs={{0,1},{1,0},{2,3},{3,2},{4,5},{5,4},{6,7},{7,6},{8,9},{9,8},{10,11... | collective-permute-start | bytes 1966088 | tf_op jit(solution)/shard_map/ppermute | solution.py:19
  12.3 2.7 collective-permute-start.3
  14.6 12.8 %collective-permute-start.2 = (f32[2,256]{1,0:T(2,128)S(1)}, f32[2,256]{1,0:T(2,128)S(1)}, u32[]{:S(2)}, u32[]{:S(2)}) collective-permute-start(f32[2,256]{1,0:T(2,128)S(1)} %pad_maximum_fusion.6), channel_id=1, source_target_pairs={{0,1},{1,0},{2,3},{3,2},{4,5},{5,4},{6,7},{7,6},{8,9},{9,8},{10,11... | collective-permute-start | bytes 6152 | tf_op jit(solution)/shard_map/ppermute | solution.py:19
  27.3 4.5 %collective-permute-start.5 = (f32[2,256]{1,0:T(2,128)S(1)}, f32[2,256]{1,0:T(2,128)S(1)}, u32[]{:S(2)}, u32[]{:S(2)}) collective-permute-start(f32[2,256]{1,0:T(2,128)S(1)} %add.248), channel_id=1, source_target_pairs={{0,2},{1,3},{2,0},{3,1},{4,6},{5,7},{6,4},{7,5},{8,10},{9,11},{10,... | collective-permute-start | bytes 6152 | tf_op jit(solution)/shard_map/ppermute | solution.py:19
  31.8 8.2 %collective-permute-start.6 = (bf16[256,2048]{1,0:T(8,128)(2,1)S(1)}, bf16[256,2048]{1,0:T(8,128)(2,1)S(1)}, u32[]{:S(2)}, u32[]{:S(2)}) collective-permute-start(bf16[256,2048]{1,0:T(8,128)(2,1)S(1)} %collective-permute-done.4), channel_id=1, source_target_pairs={{0,4},{4,0},{8,12},{12,8},{1,5},{5,1},{9,13},{13,9},{2,6},{6,2},{1... | collective-permute-start | bytes 3145736 | tf_op jit(solution)/shard_map/ppermute | solution.py:19
  32.4 18.3 %collective-permute-start.10 = (bf16[2,1,64,1280]{3,2,1,0:T(8,128)(2,1)S(1)}, bf16[2,1,64,1280]{3,2,1,0:T(8,128)(2,1)S(1)}, u32[]{:S(2)}, u32[]{:S(2)}) collective-permute-start(bf16[2,1,64,1280]{3,2,1,0:T(8,128)(2,1)S(1)} %get-tuple-element.196), channel_id=1, source_target_pairs={{0,2},{1,3},{2,0},{3,1},{4,6},{5,7},{6,4},{7,5},{8,10},{9,11},{10,... | collective-permute-start | bytes 983048 | tf_op jit(solution)/shard_map/ppermute | solution.py:19
  35.2 23.4 %collective-permute-start.9 = (bf16[2,2,64,1280]{3,2,1,0:T(8,128)(2,1)S(1)}, bf16[2,2,64,1280]{3,2,1,0:T(8,128)(2,1)S(1)}, u32[]{:S(2)}, u32[]{:S(2)}) collective-permute-start(bf16[2,2,64,1280]{3,2,1,0:T(8,128)(2,1)S(1)} %convolution_convert_fusion.2), channel_id=1, source_target_pairs={{0,1},{1,0},{2,3},{3,2},{4,5},{5,4},{6,7},{7,6},{8,9},{9,8},{10,11... | collective-permute-start | bytes 1966088 | tf_op jit(solution)/shard_map/ppermute | solution.py:19
  36.9 25.2 %collective-permute-start.8 = (bf16[256,2048]{1,0:T(8,128)(2,1)S(1)}, bf16[256,2048]{1,0:T(8,128)(2,1)}, u32[]{:S(2)}, u32[]{:S(2)}) collective-permute-start(bf16[256,2048]{1,0:T(8,128)(2,1)S(1)} %bitcast.275), channel_id=1, source_target_pairs={{0,8},{4,12},{8,0},{12,4},{1,9},{5,13},{9,1},{13,5},{2,10},{6,14},... | collective-permute-start | bytes 3145736 | tf_op jit(solution)/shard_map/ppermute | solution.py:19
  41.7 30.2 %collective-permute-start.7 = (bf16[2,2,64,1280]{3,2,1,0:T(8,128)(2,1)S(1)}, bf16[2,2,64,1280]{3,2,1,0:T(8,128)(2,1)S(1)}, u32[]{:S(2)}, u32[]{:S(2)}) collective-permute-start(bf16[2,2,64,1280]{3,2,1,0:T(8,128)(2,1)S(1)} %convolution_convert_fusion.1), channel_id=1, source_target_pairs={{0,1},{1,0},{2,3},{3,2},{4,5},{5,4},{6,7},{7,6},{8,9},{9,8},{10,11... | collective-permute-start | bytes 1966088 | tf_op jit(solution)/shard_map/ppermute | solution.py:19
  50.7 55.6 %copy-start = (bf16[2,1,64,1280]{3,2,1,0:T(8,128)(2,1)}, bf16[2,1,64,1280]{3,2,1,0:T(8,128)(2,1)S(1)}, u32[]{:S(2)}) copy-start(bf16[2,1,64,1280]{3,2,1,0:T(8,128)(2,1)S(1)} %collective-permute-done.10) | copy-start | bytes 983044
  62.0 15.6 %collective-permute-start.13 = (bf16[256,2048]{1,0:T(8,128)(2,1)}, bf16[256,2048]{1,0:T(8,128)(2,1)}, u32[]{:S(2)}, u32[]{:S(2)}) collective-permute-start(bf16[256,2048]{1,0:T(8,128)(2,1)} %collective-permute-done.8), channel_id=1, source_target_pairs={{0,4},{4,0},{8,12},{12,8},{1,5},{5,1},{9,13},{13,9},{2,6},{6,2},{1... | collective-permute-start | bytes 3145736 | tf_op jit(solution)/shard_map/ppermute | solution.py:19
  62.2 10.6 %collective-permute-start.15 = (f32[2,256]{1,0:T(2,128)S(1)}, f32[2,256]{1,0:T(2,128)S(1)}, u32[]{:S(2)}, u32[]{:S(2)}) collective-permute-start(f32[2,256]{1,0:T(2,128)S(1)} %add.253), channel_id=1, source_target_pairs={{0,8},{4,12},{8,0},{12,4},{1,9},{5,13},{9,1},{13,5},{2,10},{6,14},... | collective-permute-start | bytes 6152 | tf_op jit(solution)/shard_map/ppermute | solution.py:19
  72.8 4.5 %collective-permute-start.16 = (f32[2,256]{1,0:T(2,128)S(1)}, f32[2,256]{1,0:T(2,128)S(1)}, u32[]{:S(2)}, u32[]{:S(2)}) collective-permute-start(f32[2,256]{1,0:T(2,128)S(1)} %collective-permute-done.15), channel_id=1, source_target_pairs={{0,4},{4,0},{8,12},{12,8},{1,5},{5,1},{9,13},{13,9},{2,6},{6,2},{1... | collective-permute-start | bytes 6152 | tf_op jit(solution)/shard_map/ppermute | solution.py:19
  72.8 4.6 %collective-permute-start.14 = (f32[2,256]{1,0:T(2,128)S(1)}, f32[2,256]{1,0:T(2,128)S(1)}, u32[]{:S(2)}, u32[]{:S(2)}) collective-permute-start(f32[2,256]{1,0:T(2,128)S(1)} %add.253), channel_id=1, source_target_pairs={{0,4},{4,0},{8,12},{12,8},{1,5},{5,1},{9,13},{13,9},{2,6},{6,2},{1... | collective-permute-start | bytes 6152 | tf_op jit(solution)/shard_map/ppermute | solution.py:19
  74.3 25.8 %collective-permute-start.12 = (bf16[2,1,64,1280]{3,2,1,0:T(8,128)(2,1)}, bf16[2,1,64,1280]{3,2,1,0:T(8,128)(2,1)S(1)}, u32[]{:S(2)}, u32[]{:S(2)}) collective-permute-start(bf16[2,1,64,1280]{3,2,1,0:T(8,128)(2,1)} %get-tuple-element.193), channel_id=1, source_target_pairs={{0,2},{1,3},{2,0},{3,1},{4,6},{5,7},{6,4},{7,5},{8,10},{9,11},{10,... | collective-permute-start | bytes 983048 | tf_op jit(solution)/shard_map/ppermute | solution.py:19
  75.7 30.5 %collective-permute-start.11 = (bf16[2,1,64,1280]{3,2,1,0:T(8,128)(2,1)}, bf16[2,1,64,1280]{3,2,1,0:T(8,128)(2,1)S(1)}, u32[]{:S(2)}, u32[]{:S(2)}) collective-permute-start(bf16[2,1,64,1280]{3,2,1,0:T(8,128)(2,1)} %get-tuple-element.194), channel_id=1, source_target_pairs={{0,2},{1,3},{2,0},{3,1},{4,6},{5,7},{6,4},{7,5},{8,10},{9,11},{10,... | collective-permute-start | bytes 983048 | tf_op jit(solution)/shard_map/ppermute | solution.py:19
  84.6 39.1 %collective-permute-start.20 = (bf16[2,2,64,1280]{3,2,1,0:T(8,128)(2,1)}, bf16[2,2,64,1280]{3,2,1,0:T(8,128)(2,1)}, u32[]{:S(2)}, u32[]{:S(2)}) collective-permute-start(bf16[2,2,64,1280]{3,2,1,0:T(8,128)(2,1)} %convolution_convert_fusion), channel_id=1, source_target_pairs={{0,1},{1,0},{2,3},{3,2},{4,5},{5,4},{6,7},{7,6},{8,9},{9,8},{10,11... | collective-permute-start | bytes 1966088 | tf_op jit(solution)/shard_map/ppermute | solution.py:19
  100.2 23.5 %copy-start.2 = (bf16[2,1,64,1280]{3,2,1,0:T(8,128)(2,1)}, bf16[2,1,64,1280]{3,2,1,0:T(8,128)(2,1)S(1)}, u32[]{:S(2)}) copy-start(bf16[2,1,64,1280]{3,2,1,0:T(8,128)(2,1)S(1)} %collective-permute-done.12) | copy-start | bytes 983044
  106.2 19.7 %copy-start.5 = (bf16[2,1,64,1280]{3,2,1,0:T(8,128)(2,1)}, bf16[2,1,64,1280]{3,2,1,0:T(8,128)(2,1)S(1)}, u32[]{:S(2)}) copy-start(bf16[2,1,64,1280]{3,2,1,0:T(8,128)(2,1)S(1)} %collective-permute-done.11) | copy-start | bytes 983044
  106.5 19.5 %copy-start.7 = (bf16[256,256]{1,0:T(8,128)(2,1)}, bf16[256,256]{1,0:T(8,128)(2,1)S(1)}, u32[]{:S(2)}) copy-start(bf16[256,256]{1,0:T(8,128)(2,1)S(1)} %shard_map.140.rest_0_) | copy-start | bytes 393220
  106.5 15.9 %collective-permute-start.17 = (bf16[256,256]{1,0:T(8,128)(2,1)S(1)}, bf16[256,256]{1,0:T(8,128)(2,1)S(1)}, u32[]{:S(2)}, u32[]{:S(2)}) collective-permute-start(bf16[256,256]{1,0:T(8,128)(2,1)S(1)} %shard_map.140.rest_0_), channel_id=1, source_target_pairs={{0,1},{1,0},{2,3},{3,2},{4,5},{5,4},{6,7},{7,6},{8,9},{9,8},{10,11... | collective-permute-start | bytes 393224 | tf_op jit(solution)/shard_map/ppermute | solution.py:23
  106.5 16.5 %collective-permute-start.18 = (bf16[256,256]{1,0:T(8,128)(2,1)S(1)}, bf16[256,256]{1,0:T(8,128)(2,1)S(1)}, u32[]{:S(2)}, u32[]{:S(2)}) collective-permute-start(bf16[256,256]{1,0:T(8,128)(2,1)S(1)} %shard_map.140.rest_0_), channel_id=1, source_target_pairs={{0,2},{1,3},{2,0},{3,1},{4,6},{5,7},{6,4},{7,5},{8,10},{9,11},{10,... | collective-permute-start | bytes 393224 | tf_op jit(solution)/shard_map/ppermute | solution.py:23
  109.4 14.3 %collective-permute-start.19 = (bf16[256,256]{1,0:T(8,128)(2,1)S(1)}, bf16[256,256]{1,0:T(8,128)(2,1)}, u32[]{:S(2)}, u32[]{:S(2)}) collective-permute-start(bf16[256,256]{1,0:T(8,128)(2,1)S(1)} %shard_map.140.rest_0_), channel_id=1, source_target_pairs={{0,3},{1,2},{2,1},{3,0},{4,7},{5,6},{6,5},{7,4},{8,11},{9,10},{10,... | collective-permute-start | bytes 393224 | tf_op jit(solution)/shard_map/ppermute | solution.py:23
  126.0 16.6 %collective-permute-start.22 = (bf16[2,1,64,1280]{3,2,1,0:T(8,128)(2,1)}, bf16[2,1,64,1280]{3,2,1,0:T(8,128)(2,1)}, u32[]{:S(2)}, u32[]{:S(2)}) collective-permute-start(bf16[2,1,64,1280]{3,2,1,0:T(8,128)(2,1)} %get-tuple-element.191), channel_id=1, source_target_pairs={{0,2},{1,3},{2,0},{3,1},{4,6},{5,7},{6,4},{7,5},{8,10},{9,11},{10,... | collective-permute-start | bytes 983048 | tf_op jit(solution)/shard_map/ppermute | solution.py:19
  138.5 31.1 %collective-permute-start.21 = (bf16[256,1024]{1,0:T(8,128)(2,1)S(1)}, bf16[256,1024]{1,0:T(8,128)(2,1)}, u32[]{:S(2)}, u32[]{:S(2)}) collective-permute-start(bf16[256,1024]{1,0:T(8,128)(2,1)S(1)} %shard_map.141), channel_id=1, source_target_pairs={{0,1},{1,0},{2,3},{3,2},{4,5},{5,4},{6,7},{7,6},{8,9},{9,8},{10,11... | collective-permute-start | bytes 1572872 | tf_op jit(solution)/shard_map/ppermute | solution.py:19
  144.7 17.3 %collective-permute-start.23 = (bf16[256,256]{1,0:T(8,128)(2,1)S(1)}, bf16[256,256]{1,0:T(8,128)(2,1)S(1)}, u32[]{:S(2)}, u32[]{:S(2)}) collective-permute-start(bf16[256,256]{1,0:T(8,128)(2,1)S(1)} %shard_map.142.rest_0_), channel_id=1, source_target_pairs={{0,1},{1,0},{2,3},{3,2},{4,5},{5,4},{6,7},{7,6},{8,9},{9,8},{10,11... | collective-permute-start | bytes 393224 | tf_op jit(solution)/shard_map/ppermute | solution.py:23
  144.8 17.2 %collective-permute-start.24 = (bf16[256,256]{1,0:T(8,128)(2,1)S(1)}, bf16[256,256]{1,0:T(8,128)(2,1)S(1)}, u32[]{:S(2)}, u32[]{:S(2)}) collective-permute-start(bf16[256,256]{1,0:T(8,128)(2,1)S(1)} %shard_map.142.rest_0_), channel_id=1, source_target_pairs={{0,2},{1,3},{2,0},{3,1},{4,6},{5,7},{6,4},{7,5},{8,10},{9,11},{10,... | collective-permute-start | bytes 393224 | tf_op jit(solution)/shard_map/ppermute | solution.py:23
  147.7 14.3 %collective-permute-start.25 = (bf16[256,256]{1,0:T(8,128)(2,1)S(1)}, bf16[256,256]{1,0:T(8,128)(2,1)S(1)}, u32[]{:S(2)}, u32[]{:S(2)}) collective-permute-start(bf16[256,256]{1,0:T(8,128)(2,1)S(1)} %shard_map.142.rest_0_), channel_id=1, source_target_pairs={{0,3},{1,2},{2,1},{3,0},{4,7},{5,6},{6,5},{7,4},{8,11},{9,10},{10,... | collective-permute-start | bytes 393224 | tf_op jit(solution)/shard_map/ppermute | solution.py:23
  163.9 7.6 %copy-start.15 = (bf16[1,1024,2048]{2,1,0:T(8,128)(2,1)S(1)}, bf16[1,1024,2048]{2,1,0:T(8,128)(2,1)}, u32[]{:S(2)}) copy-start(bf16[1,1024,2048]{2,1,0:T(8,128)(2,1)} %param.18) | copy-start | bytes 12582916
  171.5 12.1 %copy-start.19 = (bf16[1,256,2048]{2,1,0:T(8,128)(2,1)S(1)}, bf16[1,256,2048]{2,1,0:T(8,128)(2,1)}, u32[]{:S(2)}) copy-start(bf16[1,256,2048]{2,1,0:T(8,128)(2,1)} %param.13) | copy-start | bytes 3145732
  171.5 13.4 %copy-start.21 = (bf16[1,256,2048]{2,1,0:T(8,128)(2,1)S(1)}, bf16[1,256,2048]{2,1,0:T(8,128)(2,1)}, u32[]{:S(2)}) copy-start(bf16[1,256,2048]{2,1,0:T(8,128)(2,1)} %param.19) | copy-start | bytes 3145732
  183.6 27.4 %collective-permute-start.26 = (bf16[2,128,2048]{2,1,0:T(8,128)(2,1)}, bf16[2,128,2048]{2,1,0:T(8,128)(2,1)}, u32[]{:S(2)}, u32[]{:S(2)}) collective-permute-start(bf16[2,128,2048]{2,1,0:T(8,128)(2,1)} %fusion.24), channel_id=1, source_target_pairs={{0,4},{4,0},{8,12},{12,8},{1,5},{5,1},{9,13},{13,9},{2,6},{6,2},{1... | collective-permute-start | bytes 3145736 | tf_op jit(solution)/shard_map/ppermute | solution.py:19
  184.4 26.6 %collective-permute-start.27 = (bf16[256,1024]{1,0:T(8,128)(2,1)S(1)}, bf16[256,1024]{1,0:T(8,128)(2,1)}, u32[]{:S(2)}, u32[]{:S(2)}) collective-permute-start(bf16[256,1024]{1,0:T(8,128)(2,1)S(1)} %shard_map.141), channel_id=1, source_target_pairs={{0,2},{1,3},{2,0},{3,1},{4,6},{5,7},{6,4},{7,5},{8,10},{9,11},{10,... | collective-permute-start | bytes 1572872 | tf_op jit(solution)/shard_map/ppermute | solution.py:19
  185.6 34.0 %collective-permute-start.30 = (bf16[256,1024]{1,0:T(8,128)(2,1)S(1)}, bf16[256,1024]{1,0:T(8,128)(2,1)S(1)}, u32[]{:S(2)}, u32[]{:S(2)}) collective-permute-start(bf16[256,1024]{1,0:T(8,128)(2,1)S(1)} %shard_map.143), channel_id=1, source_target_pairs={{0,1},{1,0},{2,3},{3,2},{4,5},{5,4},{6,7},{7,6},{8,9},{9,8},{10,11... | collective-permute-start | bytes 1572872 | tf_op jit(solution)/shard_map/ppermute | solution.py:19
  188.1 45.1 %collective-permute-start.29 = (bf16[256,1024]{1,0:T(8,128)(2,1)S(1)}, bf16[256,1024]{1,0:T(8,128)(2,1)S(1)}, u32[]{:S(2)}, u32[]{:S(2)}) collective-permute-start(bf16[256,1024]{1,0:T(8,128)(2,1)S(1)} %shard_map.143), channel_id=1, source_target_pairs={{0,2},{1,3},{2,0},{3,1},{4,6},{5,7},{6,4},{7,5},{8,10},{9,11},{10,... | collective-permute-start | bytes 1572872 | tf_op jit(solution)/shard_map/ppermute | solution.py:19
  192.7 21.0 %copy-start.16 = (bf16[1,1024,2048]{2,1,0:T(8,128)(2,1)S(1)}, bf16[1,1024,2048]{2,1,0:T(8,128)(2,1)}, u32[]{:S(2)}) copy-start(bf16[1,1024,2048]{2,1,0:T(8,128)(2,1)} %param.18) | copy-start | bytes 12582916
  211.0 25.4 %collective-permute-start.36 = (bf16[256,1024]{1,0:T(8,128)(2,1)}, bf16[256,1024]{1,0:T(8,128)(2,1)S(1)}, u32[]{:S(2)}, u32[]{:S(2)}) collective-permute-start(bf16[256,1024]{1,0:T(8,128)(2,1)} %collective-permute-done.27), channel_id=1, source_target_pairs={{0,1},{1,0},{2,3},{3,2},{4,5},{5,4},{6,7},{7,6},{8,9},{9,8},{10,11... | collective-permute-start | bytes 1572872 | tf_op jit(solution)/shard_map/ppermute | solution.py:19
  215.3 17.9 %collective-permute-start.28 = (bf16[1,128,2048]{2,1,0:T(8,128)(2,1)S(1)}, bf16[1,128,2048]{2,1,0:T(8,128)(2,1)S(1)}, u32[]{:S(2)}, u32[]{:S(2)}) collective-permute-start(bf16[1,128,2048]{2,1,0:T(8,128)(2,1)S(1)} %fusion.86), channel_id=1, source_target_pairs={{0,8},{4,12},{8,0},{12,4},{1,9},{5,13},{9,1},{13,5},{2,10},{6,14},... | collective-permute-start | bytes 1572872 | tf_op jit(solution)/shard_map/ppermute | solution.py:19
  216.9 1.9 collective-permute-start.31
  219.0 16.6 %collective-permute-start.33 = (bf16[1,64,2048]{2,1,0:T(8,128)(2,1)S(1)}, bf16[1,64,2048]{2,1,0:T(8,128)(2,1)S(1)}, u32[]{:S(2)}, u32[]{:S(2)}) collective-permute-start(bf16[1,64,2048]{2,1,0:T(8,128)(2,1)S(1)} %fusion.88), channel_id=1, source_target_pairs={{0,8},{4,12},{8,0},{12,4},{1,9},{5,13},{9,1},{13,5},{2,10},{6,14},... | collective-permute-start | bytes 786440 | tf_op jit(solution)/shard_map/ppermute | solution.py:19
  221.1 14.0 %collective-permute-start.34 = (bf16[2,128,2048]{2,1,0:T(8,128)(2,1)S(1)}, bf16[2,128,2048]{2,1,0:T(8,128)(2,1)S(1)}, u32[]{:S(2)}, u32[]{:S(2)}) collective-permute-start(bf16[2,128,2048]{2,1,0:T(8,128)(2,1)S(1)} %fusion.27), channel_id=1, source_target_pairs={{0,4},{4,0},{8,12},{12,8},{1,5},{5,1},{9,13},{13,9},{2,6},{6,2},{1... | collective-permute-start | bytes 3145736 | tf_op jit(solution)/shard_map/ppermute | solution.py:19
  221.7 11.6 %copy-start.23 = (bf16[1,64,2048]{2,1,0:T(8,128)(2,1)S(1)}, bf16[1,64,2048]{2,1,0:T(8,128)(2,1)}, u32[]{:S(2)}) copy-start(bf16[1,64,2048]{2,1,0:T(8,128)(2,1)} %get-tuple-element.200) | copy-start | bytes 786436
  221.7 11.6 %copy-start.24 = (bf16[1,64,2048]{2,1,0:T(8,128)(2,1)S(1)}, bf16[1,64,2048]{2,1,0:T(8,128)(2,1)}, u32[]{:S(2)}) copy-start(bf16[1,64,2048]{2,1,0:T(8,128)(2,1)} %get-tuple-element.201) | copy-start | bytes 786436
  233.2 32.8 %collective-permute-start.45 = (bf16[256,1024]{1,0:T(8,128)(2,1)S(1)}, bf16[256,1024]{1,0:T(8,128)(2,1)S(1)}, u32[]{:S(2)}, u32[]{:S(2)}) collective-permute-start(bf16[256,1024]{1,0:T(8,128)(2,1)S(1)} %collective-permute-done.29), channel_id=1, source_target_pairs={{0,1},{1,0},{2,3},{3,2},{4,5},{5,4},{6,7},{7,6},{8,9},{9,8},{10,11... | collective-permute-start | bytes 1572872 | tf_op jit(solution)/shard_map/ppermute | solution.py:19
  233.5 34.0 %collective-permute-start.32 = (bf16[2,64,2048]{2,1,0:T(8,128)(2,1)S(1)}, bf16[2,64,2048]{2,1,0:T(8,128)(2,1)S(1)}, u32[]{:S(2)}, u32[]{:S(2)}) collective-permute-start(bf16[2,64,2048]{2,1,0:T(8,128)(2,1)S(1)} %add_convert_fusion.1), channel_id=1, source_target_pairs={{0,16},{16,0},{1,17},{17,1},{2,18},{18,2},{3,19},{19,3},{4,20},{20... | collective-permute-start | bytes 1572872 | tf_op jit(solution)/shard_map/ppermute | solution.py:28
  237.1 4.2 %collective-permute-start.37 = (bf16[2,64,2048]{2,1,0:T(8,128)(2,1)S(1)}, bf16[2,64,2048]{2,1,0:T(8,128)(2,1)S(1)}, u32[]{:S(2)}, u32[]{:S(2)}) collective-permute-start(bf16[2,64,2048]{2,1,0:T(8,128)(2,1)S(1)} %fusion.33), channel_id=1, source_target_pairs={{0,4},{4,0},{8,12},{12,8},{1,5},{5,1},{9,13},{13,9},{2,6},{6,2},{1... | collective-permute-start | bytes 1572872 | tf_op jit(solution)/shard_map/ppermute | solution.py:19
  238.7 14.8 %collective-permute-start.39 = (bf16[1,128,2048]{2,1,0:T(8,128)(2,1)S(1)}, bf16[1,128,2048]{2,1,0:T(8,128)(2,1)S(1)}, u32[]{:S(2)}, u32[]{:S(2)}) collective-permute-start(bf16[1,128,2048]{2,1,0:T(8,128)(2,1)S(1)} %fusion.87), channel_id=1, source_target_pairs={{0,8},{4,12},{8,0},{12,4},{1,9},{5,13},{9,1},{13,5},{2,10},{6,14},... | collective-permute-start | bytes 1572872 | tf_op jit(solution)/shard_map/ppermute | solution.py:19
  240.3 2.8 collective-permute-start.40
  241.3 26.8 %collective-permute-start.35 = (bf16[1,64,2048]{2,1,0:T(8,128)(2,1)S(1)}, bf16[1,64,2048]{2,1,0:T(8,128)(2,1)S(1)}, u32[]{:S(2)}, u32[]{:S(2)}) collective-permute-start(bf16[1,64,2048]{2,1,0:T(8,128)(2,1)S(1)} %add_convert_fusion.9), channel_id=1, source_target_pairs={{0,16},{16,0},{1,17},{17,1},{2,18},{18,2},{3,19},{19,3},{4,20},{20... | collective-permute-start | bytes 786440 | tf_op jit(solution)/shard_map/ppermute | solution.py:28
  243.0 12.1 %copy-start.22 = (bf16[1,64,2048]{2,1,0:T(8,128)(2,1)S(1)}, bf16[1,64,2048]{2,1,0:T(8,128)(2,1)}, u32[]{:S(2)}) copy-start(bf16[1,64,2048]{2,1,0:T(8,128)(2,1)} %get-tuple-element.199) | copy-start | bytes 786436
  243.1 16.0 %collective-permute-start.38 = (bf16[1,64,2048]{2,1,0:T(8,128)(2,1)S(1)}, bf16[1,64,2048]{2,1,0:T(8,128)(2,1)S(1)}, u32[]{:S(2)}, u32[]{:S(2)}) collective-permute-start(bf16[1,64,2048]{2,1,0:T(8,128)(2,1)S(1)} %fusion.89), channel_id=1, source_target_pairs={{0,8},{4,12},{8,0},{12,4},{1,9},{5,13},{9,1},{13,5},{2,10},{6,14},... | collective-permute-start | bytes 786440 | tf_op jit(solution)/shard_map/ppermute | solution.py:19
  253.5 10.8 %collective-permute-start.43 = (bf16[1,64,2048]{2,1,0:T(8,128)(2,1)S(1)}, bf16[1,64,2048]{2,1,0:T(8,128)(2,1)S(1)}, u32[]{:S(2)}, u32[]{:S(2)}) collective-permute-start(bf16[1,64,2048]{2,1,0:T(8,128)(2,1)S(1)} %fusion.90), channel_id=1, source_target_pairs={{0,8},{4,12},{8,0},{12,4},{1,9},{5,13},{9,1},{13,5},{2,10},{6,14},... | collective-permute-start | bytes 786440 | tf_op jit(solution)/shard_map/ppermute | solution.py:19
  259.1 30.4 %collective-permute-start.42 = (bf16[2,64,2048]{2,1,0:T(8,128)(2,1)S(1)}, bf16[2,64,2048]{2,1,0:T(8,128)(2,1)S(1)}, u32[]{:S(2)}, u32[]{:S(2)}) collective-permute-start(bf16[2,64,2048]{2,1,0:T(8,128)(2,1)S(1)} %add_convert_fusion), channel_id=1, source_target_pairs={{0,16},{16,0},{1,17},{17,1},{2,18},{18,2},{3,19},{19,3},{4,20},{20... | collective-permute-start | bytes 1572872 | tf_op jit(solution)/shard_map/ppermute | solution.py:28
  264.3 15.3 %collective-permute-start.41 = (bf16[1,64,2048]{2,1,0:T(8,128)(2,1)S(1)}, bf16[1,64,2048]{2,1,0:T(8,128)(2,1)S(1)}, u32[]{:S(2)}, u32[]{:S(2)}) collective-permute-start(bf16[1,64,2048]{2,1,0:T(8,128)(2,1)S(1)} %add_convert_fusion.8), channel_id=1, source_target_pairs={{0,16},{16,0},{1,17},{17,1},{2,18},{18,2},{3,19},{19,3},{4,20},{20... | collective-permute-start | bytes 786440 | tf_op jit(solution)/shard_map/ppermute | solution.py:28
  266.7 13.2 %collective-permute-start.46 = (bf16[2,64,2048]{2,1,0:T(8,128)(2,1)S(1)}, bf16[2,64,2048]{2,1,0:T(8,128)(2,1)S(1)}, u32[]{:S(2)}, u32[]{:S(2)}) collective-permute-start(bf16[2,64,2048]{2,1,0:T(8,128)(2,1)S(1)} %fusion.39), channel_id=1, source_target_pairs={{0,4},{4,0},{8,12},{12,8},{1,5},{5,1},{9,13},{13,9},{2,6},{6,2},{1... | collective-permute-start | bytes 1572872 | tf_op jit(solution)/shard_map/ppermute | solution.py:19
  267.6 21.9 %collective-permute-start.44 = (bf16[1,64,2048]{2,1,0:T(8,128)(2,1)S(1)}, bf16[1,64,2048]{2,1,0:T(8,128)(2,1)S(1)}, u32[]{:S(2)}, u32[]{:S(2)}) collective-permute-start(bf16[1,64,2048]{2,1,0:T(8,128)(2,1)S(1)} %add_convert_fusion.7), channel_id=1, source_target_pairs={{0,16},{16,0},{1,17},{17,1},{2,18},{18,2},{3,19},{19,3},{4,20},{20... | collective-permute-start | bytes 786440 | tf_op jit(solution)/shard_map/ppermute | solution.py:28
  280.1 6.4 %collective-permute-start.47 = (bf16[1,64,2048]{2,1,0:T(8,128)(2,1)S(1)}, bf16[1,64,2048]{2,1,0:T(8,128)(2,1)S(1)}, u32[]{:S(2)}, u32[]{:S(2)}) collective-permute-start(bf16[1,64,2048]{2,1,0:T(8,128)(2,1)S(1)} %fusion.91), channel_id=1, source_target_pairs={{0,8},{4,12},{8,0},{12,4},{1,9},{5,13},{9,1},{13,5},{2,10},{6,14},... | collective-permute-start | bytes 786440 | tf_op jit(solution)/shard_map/ppermute | solution.py:19
  286.6 6.4 %collective-permute-start.48 = (bf16[1,64,2048]{2,1,0:T(8,128)(2,1)S(1)}, bf16[1,64,2048]{2,1,0:T(8,128)(2,1)S(1)}, u32[]{:S(2)}, u32[]{:S(2)}) collective-permute-start(bf16[1,64,2048]{2,1,0:T(8,128)(2,1)S(1)} %add_convert_fusion.6), channel_id=1, source_target_pairs={{0,16},{16,0},{1,17},{17,1},{2,18},{18,2},{3,19},{19,3},{4,20},{20... | collective-permute-start | bytes 786440 | tf_op jit(solution)/shard_map/ppermute | solution.py:28
  (21 other events, 53.6 us)
